TPU v7x, 32 devices: a whole 2x2x4 slice. The times are simulated.
32 devices in a mesh: dp: 2 (over x), seq: 16 (over z, y, core).
Axes of the slice: x: 2, y: 2, z: 4, core: 2. Of those that a mesh axis runs over, the one named last changes fastest.
Arguments:
- inputs: bfloat16 [4, 2048, 512], P('dp', 'seq'), may hold values from -6 to 6
- grad_out: bfloat16 [4, 2048, 512], P('dp', 'seq'), may hold values from -6 to 6
- seg_ids: int32 [4, 2048], P('dp', 'seq'), may hold values from 0 to 3, never falling along the last dimension, each value on 1 to 1024 neighbouring positions
- pad_mask: int32 [4, 2048], P('dp', 'seq'), may hold values 0 or 1
- w_query: bfloat16 [262144], P(('dp', 'seq')), may hold values from -1 to 1
- w_key: bfloat16 [262144], P(('dp', 'seq')), may hold values from -0.25 to 0.25
- w_value: bfloat16 [262144], P(('dp', 'seq')), may hold values from -0.25 to 0.25
- w_control: bfloat16 [262144], P(('dp', 'seq')), may hold values from -0.5 to 0.5
- w_out: bfloat16 [262144], P(('dp', 'seq')), may hold values from -0.75 to 0.75
- w_up: bfloat16 [1048576], P(('dp', 'seq')), may hold values from -0.25 to 0.25
- w_down: bfloat16 [1048576], P(('dp', 'seq')), may hold values from -0.125 to 0.125
- gain_attn: float32 [512], replicated, may hold values from 0.5 to 1.5
- gain_ffn: float32 [512], replicated, may hold values from 0.5 to 1.5
Outputs:
- output: bfloat16 [4, 2048, 512], P('dp', 'seq')
- grad_inputs: bfloat16 [4, 2048, 512], P('dp', 'seq')
- grad_query: float32 [262144], P(('dp', 'seq'))
- grad_key: float32 [262144], P(('dp', 'seq'))
- grad_value: float32 [262144], P(('dp', 'seq'))
- grad_control: float32 [262144], P(('dp', 'seq'))
- grad_outproj: float32 [262144], P(('dp', 'seq'))
- grad_up: float32 [1048576], P(('dp', 'seq'))
- grad_down: float32 [1048576], P(('dp', 'seq'))
- grad_gain_attn: float32 [512], replicated
- grad_gain_ffn: float32 [512], replicated
Inputs may be any that keep to these rules, and one draw needn't show every extreme that they name: `seg_ids`: document ids start at 0 and never fall along a sequence; every id up to 3 is used; each document has 1 to 1024 tokens and one has exactly 1024.
All inputs are finite; a program needn't handle non-finite values. No bound on the sum of `pad_mask` on one device may be relied on, other than what follows from the above.
Results may differ from a plain program's by a relative error of at most 0.012.
The roundings to bfloat16 on the way count: a program that leaves them out, or rounds other values in their place, can miss the bound.
Values may be sent and summed in bfloat16 or wider, within the bound.
A program may use at most 128 MiB of HBM per device.

v0:
```python
import math

import jax
import jax.numpy as jnp
from jax import lax
from jax.sharding import PartitionSpec as P

D = 512
H = 8
E = 64
S = 64
FF = 2048
HS = 512


epsilon = 1e-05
highest = lax.Precision.HIGHEST


def carried_in(array, axis, combine, identity, reverse):
    peers, position = (lax.axis_size(axis), lax.axis_index(axis))
    everything = jax.tree.map(lambda part: lax.all_gather(part, axis), array)
    start = jax.tree.map(
        lambda part, zero: jnp.broadcast_to(jnp.asarray(zero, part.dtype), part.shape),
        array,
        identity,
    )

    def step(k, before):
        at = peers - 1 - k if reverse else k
        reached = at > position if reverse else at < position
        new = combine(before, jax.tree.map(lambda part: part[at], everything))
        return jax.tree.map(lambda a, b: jnp.where(reached, a, b), new, before)

    return lax.fori_loop(0, peers, step, start)


def block_mix(q_rows, k_rows, v_rows, control, seg_rows, pad_rows, kv_in, z_in, seg_in):
    length_rows = seg_rows.shape[0]
    weight = jnp.exp(control) * pad_rows[:, None, None]
    places = jnp.arange(length_rows)
    same_doc = jnp.where(
        (seg_rows[:, None] == seg_rows[None, :]) & (places[:, None] >= places[None, :]), 1.0, 0.0
    ).astype(control.dtype)
    carry_use = jnp.where(seg_rows == seg_in, 1.0, 0.0).astype(control.dtype)[:, None, None]
    pair_dot = jnp.einsum("thd,ihd->hti", q_rows, k_rows, precision=highest) * same_doc[None]
    numerator = jnp.einsum("hti,ihs->ths", pair_dot, weight, precision=highest)
    numerator = numerator + carry_use * jnp.einsum(
        "thd,hsd->ths", q_rows, kv_in[0], precision=highest
    )
    totals = jnp.einsum("ti,ihs->ths", same_doc, weight, precision=highest) + carry_use * z_in[None]
    floors = jnp.maximum(totals, 1.0)
    scores = numerator / (floors * math.sqrt(q_rows.shape[-1]))
    slot_prob = jax.nn.softmax(scores, axis=-1)
    shares = slot_prob / floors
    mixing = jnp.einsum("ths,ihs->hti", shares, weight, precision=highest) * same_doc[None]
    result = jnp.einsum("hti,ihd->thd", mixing, v_rows, precision=highest)
    return result + carry_use * jnp.einsum("ths,hsd->thd", shares, kv_in[1], precision=highest)


def block_summary(k_rows, v_rows, control, seg_rows, pad_rows):
    last_doc = jnp.where(seg_rows == seg_rows[-1], 1.0, 0.0).astype(control.dtype)
    weight = jnp.exp(control) * (pad_rows * last_doc)[:, None, None]
    key_sum = jnp.einsum("ths,thd->hsd", weight, k_rows, precision=highest)
    value_sum = jnp.einsum("ths,thd->hsd", weight, v_rows, precision=highest)
    return (jnp.stack([key_sum, value_sum]), jnp.sum(weight, axis=0))


def join_states(earlier, later):
    kv_early, z_early, seg_early = earlier
    kv_late, z_late, seg_late = later
    keep = jnp.where(seg_early == seg_late, 1.0, 0.0).astype(jnp.float32)
    vacant = seg_late < 0
    kv_join = jnp.where(vacant, kv_early, kv_late + keep * kv_early)
    z_join = jnp.where(vacant, z_early, z_late + keep * z_early)
    return (kv_join, z_join, jnp.where(vacant, seg_early, seg_late))


def normalize(values):
    center = values - jnp.mean(values, axis=-1, keepdims=True)
    scale_inv = lax.rsqrt(jnp.mean(center * center, axis=-1, keepdims=True) + epsilon)
    return (center * scale_inv, scale_inv)


def norm_back(grad_in, unit_rows, scale_inv):
    centered = grad_in - jnp.mean(grad_in, axis=-1, keepdims=True)
    return scale_inv * (
        centered - unit_rows * jnp.mean(grad_in * unit_rows, axis=-1, keepdims=True)
    )


def outer_rows(left, right):
    return lax.dot_general(
        left, right, (((0,), (0,)), ((), ())), preferred_element_type=jnp.float32
    )


def times_transposed(left, right):
    return lax.dot_general(
        left, right, (((1,), (1,)), ((), ())), preferred_element_type=jnp.float32
    )


def body(
    inputs,
    grad_out,
    seg_ids,
    pad_mask,
    w_query,
    w_key,
    w_value,
    w_control,
    w_out,
    w_up,
    w_down,
    gain_attn,
    gain_ffn,
):
    shapes = ((D, D), (D, D), (D, D), (D, HS), (D, D), (D, FF), (FF, D))

    def unfold(gathered):
        return tuple((flat_w.reshape(form_of) for flat_w, form_of in zip(gathered, shapes)))

    def micro_step(totals, slices):
        x_rows, dy_rows, seg_rows, pad_rows = slices
        fwd_mats = unfold(
            (
                lax.all_gather(w_query, ("dp", "seq"), axis=0, tiled=True),
                lax.all_gather(w_key, ("dp", "seq"), axis=0, tiled=True),
                lax.all_gather(w_value, ("dp", "seq"), axis=0, tiled=True),
                lax.all_gather(w_control, ("dp", "seq"), axis=0, tiled=True),
                lax.all_gather(w_out, ("dp", "seq"), axis=0, tiled=True),
                lax.all_gather(w_up, ("dp", "seq"), axis=0, tiled=True),
                lax.all_gather(w_down, ("dp", "seq"), axis=0, tiled=True),
            )
        )
        wq_full, wk_full, wv_full, wc_full, wo_full, wu_full, wd_full = fwd_mats
        tokens = x_rows.shape[0]
        seg_float = seg_rows.astype(jnp.float32)
        pad_float = pad_rows.astype(jnp.float32)
        x_float = x_rows.astype(jnp.float32)
        unit_one, inv_one = normalize(x_float)
        norm_one = (unit_one * gain_attn).astype(jnp.bfloat16)
        query_bf = jnp.dot(norm_one, wq_full, preferred_element_type=jnp.float32).astype(
            jnp.bfloat16
        )
        key_bf = jnp.dot(norm_one, wk_full, preferred_element_type=jnp.float32).astype(jnp.bfloat16)
        value_bf = jnp.dot(norm_one, wv_full, preferred_element_type=jnp.float32).astype(
            jnp.bfloat16
        )
        c_rows = jnp.dot(norm_one, wc_full, preferred_element_type=jnp.float32).reshape(
            tokens, H, S
        )
        q_rows = query_bf.astype(jnp.float32).reshape(tokens, H, E)
        k_rows = key_bf.astype(jnp.float32).reshape(tokens, H, E)
        v_rows = value_bf.astype(jnp.float32).reshape(tokens, H, E)

        def summarize(k_in, v_in, c_in):
            return block_summary(k_in, v_in, c_in, seg_float, pad_float)

        (kv_loc, z_loc), pull_sum = jax.vjp(summarize, k_rows, v_rows, c_rows)
        seg_last = seg_float[-1]
        kv_in, z_in, seg_in = carried_in(
            (kv_loc, z_loc, seg_last),
            "seq",
            join_states,
            (jnp.zeros_like(kv_loc), jnp.zeros_like(z_loc), jnp.full((), -1.0, jnp.float32)),
            False,
        )

        def mix_local(q_in, k_in, v_in, c_in, kv_from, z_from):
            return block_mix(q_in, k_in, v_in, c_in, seg_float, pad_float, kv_from, z_from, seg_in)

        mixed_float, pull_mix = jax.vjp(mix_local, q_rows, k_rows, v_rows, c_rows, kv_in, z_in)
        mixed_rows = mixed_float.reshape(tokens, D).astype(jnp.bfloat16)
        residual = x_float + jnp.dot(mixed_rows, wo_full, preferred_element_type=jnp.float32)
        unit_two, inv_two = normalize(residual)
        norm_two = (unit_two * gain_ffn).astype(jnp.bfloat16)
        pre_act = jnp.dot(norm_two, wu_full, preferred_element_type=jnp.float32)
        sigmoid_pre = jax.nn.sigmoid(pre_act)
        hidden = (pre_act * sigmoid_pre).astype(jnp.bfloat16)
        y_rows = (residual + jnp.dot(hidden, wd_full, preferred_element_type=jnp.float32)).astype(
            jnp.bfloat16
        )
        back_mats = unfold(
            (
                lax.all_gather(w_query, ("dp", "seq"), axis=0, tiled=True),
                lax.all_gather(w_key, ("dp", "seq"), axis=0, tiled=True),
                lax.all_gather(w_value, ("dp", "seq"), axis=0, tiled=True),
                lax.all_gather(w_control, ("dp", "seq"), axis=0, tiled=True),
                lax.all_gather(w_out, ("dp", "seq"), axis=0, tiled=True),
                lax.all_gather(w_up, ("dp", "seq"), axis=0, tiled=True),
                lax.all_gather(w_down, ("dp", "seq"), axis=0, tiled=True),
            )
        )
        wq_back, wk_back, wv_back, wc_back, wo_back, wu_back, wd_back = back_mats
        g_down = outer_rows(hidden, dy_rows)
        d_hidden = times_transposed(dy_rows, wd_back)
        d_pre = (d_hidden * sigmoid_pre * (1.0 + pre_act * (1.0 - sigmoid_pre))).astype(
            jnp.bfloat16
        )
        g_up = outer_rows(norm_two, d_pre)
        d_norm_two = times_transposed(d_pre, wu_back)
        gain_two = jnp.sum(d_norm_two * unit_two, axis=0)
        d_residual = dy_rows.astype(jnp.float32) + norm_back(
            d_norm_two * gain_ffn, unit_two, inv_two
        )
        d_attn = d_residual.astype(jnp.bfloat16)
        g_outproj = outer_rows(mixed_rows, d_attn)
        d_mixed = times_transposed(d_attn, wo_back).reshape(tokens, H, E)
        dq_one, dk_one, dv_one, dc_one, d_kv_in, d_z_in = pull_mix(d_mixed)
        g_kv, g_z, g_seg = carried_in(
            (d_kv_in, d_z_in, seg_float[0]),
            "seq",
            join_states,
            (jnp.zeros_like(d_kv_in), jnp.zeros_like(d_z_in), jnp.full((), -1.0, jnp.float32)),
            True,
        )
        matched = jnp.where(g_seg == seg_last, 1.0, 0.0).astype(jnp.float32)
        dk_two, dv_two, dc_two = pull_sum((matched * g_kv, matched * g_z))
        d_query = dq_one.reshape(tokens, D).astype(jnp.bfloat16)
        d_key = (dk_one + dk_two).reshape(tokens, D).astype(jnp.bfloat16)
        d_value = (dv_one + dv_two).reshape(tokens, D).astype(jnp.bfloat16)
        d_control = (dc_one + dc_two).reshape(tokens, HS).astype(jnp.bfloat16)
        g_query = outer_rows(norm_one, d_query)
        g_key = outer_rows(norm_one, d_key)
        g_value = outer_rows(norm_one, d_value)
        g_control = outer_rows(norm_one, d_control)
        d_norm_one = times_transposed(d_query, wq_back) + times_transposed(d_key, wk_back)
        d_norm_one = (
            d_norm_one + times_transposed(d_value, wv_back) + times_transposed(d_control, wc_back)
        )
        gain_one = jnp.sum(d_norm_one * unit_one, axis=0)
        dx_rows = (d_residual + norm_back(d_norm_one * gain_attn, unit_one, inv_one)).astype(
            jnp.bfloat16
        )
        updates = (g_query, g_key, g_value, g_control, g_outproj, g_up, g_down, gain_one, gain_two)
        new_totals = tuple((old_sum + new_term for old_sum, new_term in zip(totals, updates)))
        return (new_totals, (y_rows, dx_rows))

    start = tuple((jnp.zeros(form_of, jnp.float32) for form_of in shapes)) + (
        jnp.zeros((D,), jnp.float32),
        jnp.zeros((D,), jnp.float32),
    )
    totals, (y_all, dx_all) = lax.scan(micro_step, start, (inputs, grad_out, seg_ids, pad_mask))
    owned = (
        lax.psum_scatter(totals[0].reshape(-1), ("dp", "seq"), scatter_dimension=0, tiled=True),
        lax.psum_scatter(totals[1].reshape(-1), ("dp", "seq"), scatter_dimension=0, tiled=True),
        lax.psum_scatter(totals[2].reshape(-1), ("dp", "seq"), scatter_dimension=0, tiled=True),
        lax.psum_scatter(totals[3].reshape(-1), ("dp", "seq"), scatter_dimension=0, tiled=True),
        lax.psum_scatter(totals[4].reshape(-1), ("dp", "seq"), scatter_dimension=0, tiled=True),
        lax.psum_scatter(totals[5].reshape(-1), ("dp", "seq"), scatter_dimension=0, tiled=True),
        lax.psum_scatter(totals[6].reshape(-1), ("dp", "seq"), scatter_dimension=0, tiled=True),
    )
    gain_sums = lax.psum((totals[7], totals[8]), ("dp", "seq"))
    return (y_all, dx_all) + tuple(owned) + tuple(gain_sums)


def solution(mesh):
    in_specs = (
        P("dp", "seq", None),
        P("dp", "seq", None),
        P("dp", "seq"),
        P("dp", "seq"),
        P(("dp", "seq")),
        P(("dp", "seq")),
        P(("dp", "seq")),
        P(("dp", "seq")),
        P(("dp", "seq")),
        P(("dp", "seq")),
        P(("dp", "seq")),
        P(),
        P(),
    )
    out_specs = (
        P("dp", "seq", None),
        P("dp", "seq", None),
        P(("dp", "seq")),
        P(("dp", "seq")),
        P(("dp", "seq")),
        P(("dp", "seq")),
        P(("dp", "seq")),
        P(("dp", "seq")),
        P(("dp", "seq")),
        P(),
        P(),
    )
    return jax.shard_map(body, mesh=mesh, in_specs=in_specs, out_specs=out_specs, check_vma=False)
```

profile of v0, /device:TPU:0, one launch (start us, length us, event | category | flops | bytes accessed | tf_op | source)
XLA Modules:
  0.0 1355.8 jit_solution(9005459857510476783)
XLA Ops:
  8.1 1065.3 %while.101 = (s32[]{:T(128)}, f32[512,512]{1,0:T(8,128)}, f32[512,512]{1,0:T(8,128)}, f32[512,512]{1,0:T(8,128)}, f32[512,512]{1,0:T(8,128)}, /*index=5*/f32[512...) while((s32[]{:T(128)}, f32[512,512]{1,0:T(8,128)}, ...), condition=%wide.region_20.21_spmd.clone, body=%wide.region_0.20_spmd.clone.sunk | while | flops 4573109248 | bytes 320184928 | solution.py:245
  9.7 45.2 %all_gather.122 = bf16[262144]{0:T(1024)(128)(2,1)S(1)} all-gather(bf16[8192]{0:T(1024)(128)(2,1)} %get-tuple-element.1532), channel_id=1, replica_groups=mesh['dp'=2,'seq'=16] {'dp','seq'}, dimensions={0}, use_global_device_ids=true | all-gather | bytes 540672 | tf_op jit(solution)/shard_map/while/body/eval_jaxpr/all_gather | solution.py:130
  58.9 38.7 %all_gather.123 = bf16[262144]{0:T(1024)(128)(2,1)S(1)} all-gather(bf16[8192]{0:T(1024)(128)(2,1)} %get-tuple-element.1531), channel_id=1, replica_groups=mesh['dp'=2,'seq'=16] {'dp','seq'}, dimensions={0}, use_global_device_ids=true | all-gather | bytes 540672 | tf_op jit(solution)/shard_map/while/body/eval_jaxpr/all_gather | solution.py:129
  98.8 40.0 %all_gather.121 = bf16[262144]{0:T(1024)(128)(2,1)S(1)} all-gather(bf16[8192]{0:T(1024)(128)(2,1)S(1)} %copy-done.77), channel_id=1, replica_groups=mesh['dp'=2,'seq'=16] {'dp','seq'}, dimensions={0}, use_global_device_ids=true | all-gather | bytes 540672 | tf_op jit(solution)/shard_map/while/body/eval_jaxpr/all_gather | solution.py:131
  145.9 31.3 %all-reduce.17 = (f32[16]{0:T(128)S(1)}, f32[16]{0:T(128)}) all-reduce(f32[16]{0:T(128)S(1)} %bitcast_dynamic-update-slice_fusion.4, f32[16]{0:T(128)S(1)} %bitcast_dynamic-update-slice_fusion.5), channel_id=2, replica_groups=mesh['dp'=2,'seq'=16] {'seq'}, use_global_device_ids=true, to_apply=%add.2 | all-reduce | flops 32 | bytes 256 | tf_op jit(solution)/shard_map/while/body/eval_jaxpr/all_gather | solution.py:22
  177.2 40.3 %all_gather.125 = bf16[262144]{0:T(1024)(128)(2,1)S(1)} all-gather(bf16[8192]{0:T(1024)(128)(2,1)S(1)} %copy-done.79), channel_id=1, replica_groups=mesh['dp'=2,'seq'=16] {'dp','seq'}, dimensions={0}, use_global_device_ids=true | all-gather | bytes 540672 | tf_op jit(solution)/shard_map/while/body/eval_jaxpr/all_gather | solution.py:132
  219.8 39.0 %all_gather.124 = bf16[262144]{0:T(1024)(128)(2,1)S(1)} all-gather(bf16[8192]{0:T(1024)(128)(2,1)S(1)} %copy-done.78), channel_id=1, replica_groups=mesh['dp'=2,'seq'=16] {'dp','seq'}, dimensions={0}, use_global_device_ids=true | all-gather | bytes 540672 | tf_op jit(solution)/shard_map/while/body/eval_jaxpr/all_gather | solution.py:128
  259.5 19.5 %all-gather.15 = f32[128,64]{1,0:T(8,128)} all-gather(f32[8,64]{1,0:T(8,128)S(1)} %get-tuple-element.1301), channel_id=4, replica_groups=mesh['dp'=2,'seq'=16] {'seq'}, dimensions={0}, use_global_device_ids=true | all-gather | bytes 34816 | tf_op jit(solution)/shard_map/while/body/eval_jaxpr/all_gather | solution.py:22
  283.3 2.8 reshape.562
  286.1 4.4 reshape.561
  290.5 74.0 %while.102 = (s32[]{:T(128)}, f32[2,8,64,64]{3,2,1,0:T(8,128)S(1)}, f32[8,64]{1,0:T(8,128)S(1)}, f32[]{:T(128)}, s32[]{:T(128)}, /*index=5*/f32[16]{0:T(128)S(1)...) while((s32[]{:T(128)}, f32[2,8,64,64]{3,2,1,0:T(8,128)S(1)}, ...), condition=%wide.region_5.5_spmd.clone, body=%wide.region_4.4_spmd.clone.sunk | while | flops 330249 | bytes 792818 | solution.py:35
  387.1 20.3 %all-gather.17 = f32[128,64]{1,0:T(8,128)} all-gather(f32[8,64]{1,0:T(8,128)S(1)} %get-tuple-element.1318), channel_id=7, replica_groups=mesh['dp'=2,'seq'=16] {'seq'}, dimensions={0}, use_global_device_ids=true | all-gather | bytes 34816 | tf_op jit(solution)/shard_map/while/body/eval_jaxpr/all_gather | solution.py:22
  428.2 29.4 %all-gather.29.cloned.1.call-done = f32[32,8,64,64]{3,2,1,0:T(8,128)} async-done(((f32[2,8,64,64]{3,2,1,0:T(8,128)}), f32[32,8,64,64]{3,2,1,0:T(8,128)}) %all-gather.29.cloned.1.call-update) | async-done | bytes 4194320 | tf_op jit(solution)/shard_map/while/body/eval_jaxpr/all_gather | solution.py:22
  457.6 74.1 %while.103 = (s32[]{:T(128)}, f32[2,8,64,64]{3,2,1,0:T(8,128)S(1)}, f32[8,64]{1,0:T(8,128)S(1)}, f32[]{:T(128)}, s32[]{:T(128)}, /*index=5*/f32[16]{0:T(128)S(1)...) while((s32[]{:T(128)}, f32[2,8,64,64]{3,2,1,0:T(8,128)S(1)}, ...), condition=%wide.region_15.15_spmd.clone, body=%wide.region_14.14_spmd.clone.sunk | while | flops 330253 | bytes 792880 | solution.py:35
  544.4 40.7 %all_gather.122 = bf16[262144]{0:T(1024)(128)(2,1)S(1)} all-gather(bf16[8192]{0:T(1024)(128)(2,1)} %get-tuple-element.1532), channel_id=1, replica_groups=mesh['dp'=2,'seq'=16] {'dp','seq'}, dimensions={0}, use_global_device_ids=true | all-gather | bytes 540672 | tf_op jit(solution)/shard_map/while/body/eval_jaxpr/all_gather | solution.py:130
  589.1 38.6 %all_gather.123 = bf16[262144]{0:T(1024)(128)(2,1)S(1)} all-gather(bf16[8192]{0:T(1024)(128)(2,1)} %get-tuple-element.1531), channel_id=1, replica_groups=mesh['dp'=2,'seq'=16] {'dp','seq'}, dimensions={0}, use_global_device_ids=true | all-gather | bytes 540672 | tf_op jit(solution)/shard_map/while/body/eval_jaxpr/all_gather | solution.py:129
  628.8 40.2 %all_gather.121 = bf16[262144]{0:T(1024)(128)(2,1)S(1)} all-gather(bf16[8192]{0:T(1024)(128)(2,1)S(1)} %copy-done.77), channel_id=1, replica_groups=mesh['dp'=2,'seq'=16] {'dp','seq'}, dimensions={0}, use_global_device_ids=true | all-gather | bytes 540672 | tf_op jit(solution)/shard_map/while/body/eval_jaxpr/all_gather | solution.py:131
  676.1 31.2 %all-reduce.17 = (f32[16]{0:T(128)S(1)}, f32[16]{0:T(128)}) all-reduce(f32[16]{0:T(128)S(1)} %bitcast_dynamic-update-slice_fusion.4, f32[16]{0:T(128)S(1)} %bitcast_dynamic-update-slice_fusion.5), channel_id=2, replica_groups=mesh['dp'=2,'seq'=16] {'seq'}, use_global_device_ids=true, to_apply=%add.2 | all-reduce | flops 32 | bytes 256 | tf_op jit(solution)/shard_map/while/body/eval_jaxpr/all_gather | solution.py:22
  707.3 40.2 %all_gather.125 = bf16[262144]{0:T(1024)(128)(2,1)S(1)} all-gather(bf16[8192]{0:T(1024)(128)(2,1)S(1)} %copy-done.79), channel_id=1, replica_groups=mesh['dp'=2,'seq'=16] {'dp','seq'}, dimensions={0}, use_global_device_ids=true | all-gather | bytes 540672 | tf_op jit(solution)/shard_map/while/body/eval_jaxpr/all_gather | solution.py:132
  749.8 39.2 %all_gather.124 = bf16[262144]{0:T(1024)(128)(2,1)S(1)} all-gather(bf16[8192]{0:T(1024)(128)(2,1)S(1)} %copy-done.78), channel_id=1, replica_groups=mesh['dp'=2,'seq'=16] {'dp','seq'}, dimensions={0}, use_global_device_ids=true | all-gather | bytes 540672 | tf_op jit(solution)/shard_map/while/body/eval_jaxpr/all_gather | solution.py:128
  789.8 19.1 %all-gather.15 = f32[128,64]{1,0:T(8,128)} all-gather(f32[8,64]{1,0:T(8,128)S(1)} %get-tuple-element.1301), channel_id=4, replica_groups=mesh['dp'=2,'seq'=16] {'seq'}, dimensions={0}, use_global_device_ids=true | all-gather | bytes 34816 | tf_op jit(solution)/shard_map/while/body/eval_jaxpr/all_gather | solution.py:22
  813.2 2.8 reshape.562
  816.0 4.4 reshape.561
  820.4 74.0 %while.102 = (s32[]{:T(128)}, f32[2,8,64,64]{3,2,1,0:T(8,128)S(1)}, f32[8,64]{1,0:T(8,128)S(1)}, f32[]{:T(128)}, s32[]{:T(128)}, /*index=5*/f32[16]{0:T(128)S(1)...) while((s32[]{:T(128)}, f32[2,8,64,64]{3,2,1,0:T(8,128)S(1)}, ...), condition=%wide.region_5.5_spmd.clone, body=%wide.region_4.4_spmd.clone.sunk | while | flops 330249 | bytes 792818 | solution.py:35
  917.0 20.7 %all-gather.17 = f32[128,64]{1,0:T(8,128)} all-gather(f32[8,64]{1,0:T(8,128)S(1)} %get-tuple-element.1318), channel_id=7, replica_groups=mesh['dp'=2,'seq'=16] {'seq'}, dimensions={0}, use_global_device_ids=true | all-gather | bytes 34816 | tf_op jit(solution)/shard_map/while/body/eval_jaxpr/all_gather | solution.py:22
  955.7 5.0 select_add_fusion.8
  960.7 27.2 %all-gather.29.cloned.1.call-done = f32[32,8,64,64]{3,2,1,0:T(8,128)} async-done(((f32[2,8,64,64]{3,2,1,0:T(8,128)}), f32[32,8,64,64]{3,2,1,0:T(8,128)}) %all-gather.29.cloned.1.call-update) | async-done | bytes 4194320 | tf_op jit(solution)/shard_map/while/body/eval_jaxpr/all_gather | solution.py:22
  987.9 74.1 %while.103 = (s32[]{:T(128)}, f32[2,8,64,64]{3,2,1,0:T(8,128)S(1)}, f32[8,64]{1,0:T(8,128)S(1)}, f32[]{:T(128)}, s32[]{:T(128)}, /*index=5*/f32[16]{0:T(128)S(1)...) while((s32[]{:T(128)}, f32[2,8,64,64]{3,2,1,0:T(8,128)S(1)}, ...), condition=%wide.region_15.15_spmd.clone, body=%wide.region_14.14_spmd.clone.sunk | while | flops 330253 | bytes 792880 | solution.py:35
  1082.5 2.9 copy.71
  1085.4 5.3 copy.72
  1091.4 40.4 %all-reduce.14 = (f32[512]{0:T(512)}, f32[512]{0:T(512)}) all-reduce(f32[512]{0:T(512)S(1)} %copy-done.92, f32[512]{0:T(512)S(1)} %copy-done.89), channel_id=1, replica_groups=mesh['dp'=2,'seq'=16] {'dp','seq'}, use_global_device_ids=true, to_apply=%region_28.29 | all-reduce | flops 1024 | bytes 8192 | tf_op jit(solution)/shard_map/psum | solution.py:255
  1131.8 206.6 %all-reduce.20.cloned.1.call-done = (f32[262144]{0:T(1024)}, f32[262144]{0:T(1024)}, f32[262144]{0:T(1024)}, f32[262144]{0:T(1024)}, f32[262144]{0:T(1024)}, /*index=5*/f32[1048576]{0:T(1024)}, f32[1048576]{0:T(1024)}) async-done(((f32[262144]{0:T(1024)}, f32[262144]{0:T(1024)}, f32[262144]{0:T(1024)}, f32[262144]{0:T(1024)}, f32[262144]{0:T(1024)}, /*index=5*/f32[1048576]{0:T(1024)}, f32[1048576]{0:T(1024)}), ...) | async-done | bytes 13631504
  (824 shorter events, 333.1 us)
Async XLA Ops:
  8.1 89.8 %copy-start = (bf16[2,128,512]{2,1,0:T(8,128)(2,1)S(1)}, bf16[2,128,512]{2,1,0:T(8,128)(2,1)}, u32[]{:S(2)}) copy-start(bf16[2,128,512]{2,1,0:T(8,128)(2,1)} %get-tuple-element.1526) | copy-start | bytes 786436 | tf_op jit(solution)/shard_map/while
  8.1 89.8 %copy-start.63 = (f32[512]{0:T(512)S(1)}, f32[512]{0:T(512)}, u32[]{:S(2)}) copy-start(f32[512]{0:T(512)} %get-tuple-element.1527) | copy-start | bytes 6148 | tf_op jit(solution)/shard_map/while
  8.1 90.6 %copy-start.77 = (bf16[8192]{0:T(1024)(128)(2,1)S(1)}, bf16[8192]{0:T(1024)(128)(2,1)}, u32[]{:S(2)}) copy-start(bf16[8192]{0:T(1024)(128)(2,1)} %get-tuple-element.1529) | copy-start | bytes 49156 | tf_op jit(solution)/shard_map/while
  8.2 131.1 %copy-start.93 = (s32[2,128]{1,0:T(2,128)S(1)}, s32[2,128]{1,0:T(2,128)}, u32[]{:S(2)}) copy-start(s32[2,128]{1,0:T(2,128)} %get-tuple-element.1528) | copy-start | bytes 3076 | tf_op jit(solution)/shard_map/while
  8.2 131.7 %copy-start.94 = (s32[2,128]{1,0:T(2,128)S(1)}, s32[2,128]{1,0:T(2,128)}, u32[]{:S(2)}) copy-start(s32[2,128]{1,0:T(2,128)} %get-tuple-element.1530) | copy-start | bytes 3076 | tf_op jit(solution)/shard_map/while
  8.2 275.1 %all-gather.27.cloned.1.call-start = ((), (), s32[]{:S(2)}) async-start(), calls=%async_computation.3 | async-start | bytes 2162688 | tf_op jit(solution)/shard_map/while/body/eval_jaxpr/all_gather | solution.py:133
  8.9 277.2 %all-gather.25.cloned.1.call-start = ((), (), s32[]{:S(2)}) async-start(), calls=%async_computation.2 | async-start | bytes 2162688 | tf_op jit(solution)/shard_map/while/body/eval_jaxpr/all_gather | solution.py:193
  9.7 280.9 %all-gather.23.cloned.1.call-start = ((), (), s32[]{:S(2)}) async-start(), calls=%async_computation.1 | async-start | bytes 8912896 | tf_op jit(solution)/shard_map/while/body/eval_jaxpr/all_gather | solution.py:22
  55.3 85.3 %copy-start.12 = (bf16[512,512]{1,0:T(8,128)(2,1)}, bf16[512,512]{1,0:T(8,128)(2,1)S(1)}, u32[]{:S(2)}) copy-start(bf16[512,512]{1,0:T(8,128)(2,1)S(1)} %reshape.557) | copy-start | bytes 1572868 | tf_op jit(solution)/shard_map/while
  56.4 202.6 %copy-start.65 = (f32[128]{0:T(128)}, f32[128]{0:T(128)S(1)}, u32[]{:S(2)}) copy-start(f32[128]{0:T(128)S(1)} %broadcast_multiply_fusion.17) | copy-start | bytes 1540 | tf_op jit(solution)/shard_map/while
  57.6 201.5 %copy-start.67 = (f32[128]{0:T(128)}, f32[128]{0:T(128)S(1)}, u32[]{:S(2)}) copy-start(f32[128]{0:T(128)S(1)} %add_rsqrt_fusion.4) | copy-start | bytes 1540 | tf_op jit(solution)/shard_map/while
  98.4 182.0 %copy-start.31 = (bf16[128,512]{0,1:T(8,128)(2,1)}, bf16[128,512]{0,1:T(8,128)(2,1)S(1)}, u32[]{:S(2)}) copy-start(bf16[128,512]{0,1:T(8,128)(2,1)S(1)} %copy.81) | copy-start | bytes 393220 | tf_op jit(solution)/shard_map/while
  138.7 81.0 %copy-start.78 = (bf16[8192]{0:T(1024)(128)(2,1)S(1)}, bf16[8192]{0:T(1024)(128)(2,1)}, u32[]{:S(2)}) copy-start(bf16[8192]{0:T(1024)(128)(2,1)} %get-tuple-element.1534) | copy-start | bytes 49156 | tf_op jit(solution)/shard_map/while
  140.6 118.8 %copy-start.85 = (f32[128]{0:T(128)}, f32[128]{0:T(128)S(1)}, u32[]{:S(2)}) copy-start(f32[128]{0:T(128)S(1)} %get-tuple-element.1295) | copy-start | bytes 1540 | tf_op jit(solution)/shard_map/while
  142.6 315.0 %all-gather.29.cloned.1.call-start = ((), (), s32[]{:S(2)}) async-start(), calls=%async_computation.4 | async-start | bytes 8912896 | tf_op jit(solution)/shard_map/while/body/eval_jaxpr/all_gather | solution.py:22
  543.1 84.8 %copy-start = (bf16[2,128,512]{2,1,0:T(8,128)(2,1)S(1)}, bf16[2,128,512]{2,1,0:T(8,128)(2,1)}, u32[]{:S(2)}) copy-start(bf16[2,128,512]{2,1,0:T(8,128)(2,1)} %get-tuple-element.1526) | copy-start | bytes 786436 | tf_op jit(solution)/shard_map/while
  543.1 84.8 %copy-start.63 = (f32[512]{0:T(512)S(1)}, f32[512]{0:T(512)}, u32[]{:S(2)}) copy-start(f32[512]{0:T(512)} %get-tuple-element.1527) | copy-start | bytes 6148 | tf_op jit(solution)/shard_map/while
  543.1 85.6 %copy-start.77 = (bf16[8192]{0:T(1024)(128)(2,1)S(1)}, bf16[8192]{0:T(1024)(128)(2,1)}, u32[]{:S(2)}) copy-start(bf16[8192]{0:T(1024)(128)(2,1)} %get-tuple-element.1529) | copy-start | bytes 49156 | tf_op jit(solution)/shard_map/while
  543.1 126.4 %copy-start.93 = (s32[2,128]{1,0:T(2,128)S(1)}, s32[2,128]{1,0:T(2,128)}, u32[]{:S(2)}) copy-start(s32[2,128]{1,0:T(2,128)} %get-tuple-element.1528) | copy-start | bytes 3076 | tf_op jit(solution)/shard_map/while
  543.1 127.0 %copy-start.94 = (s32[2,128]{1,0:T(2,128)S(1)}, s32[2,128]{1,0:T(2,128)}, u32[]{:S(2)}) copy-start(s32[2,128]{1,0:T(2,128)} %get-tuple-element.1530) | copy-start | bytes 3076 | tf_op jit(solution)/shard_map/while
  543.2 270.0 %all-gather.27.cloned.1.call-start = ((), (), s32[]{:S(2)}) async-start(), calls=%async_computation.3 | async-start | bytes 2162688 | tf_op jit(solution)/shard_map/while/body/eval_jaxpr/all_gather | solution.py:133
  543.7 272.3 %all-gather.25.cloned.1.call-start = ((), (), s32[]{:S(2)}) async-start(), calls=%async_computation.2 | async-start | bytes 2162688 | tf_op jit(solution)/shard_map/while/body/eval_jaxpr/all_gather | solution.py:193
  544.3 276.1 %all-gather.23.cloned.1.call-start = ((), (), s32[]{:S(2)}) async-start(), calls=%async_computation.1 | async-start | bytes 8912896 | tf_op jit(solution)/shard_map/while/body/eval_jaxpr/all_gather | solution.py:22
  585.4 85.4 %copy-start.12 = (bf16[512,512]{1,0:T(8,128)(2,1)}, bf16[512,512]{1,0:T(8,128)(2,1)S(1)}, u32[]{:S(2)}) copy-start(bf16[512,512]{1,0:T(8,128)(2,1)S(1)} %reshape.557) | copy-start | bytes 1572868 | tf_op jit(solution)/shard_map/while
  586.6 202.7 %copy-start.65 = (f32[128]{0:T(128)}, f32[128]{0:T(128)S(1)}, u32[]{:S(2)}) copy-start(f32[128]{0:T(128)S(1)} %broadcast_multiply_fusion.17) | copy-start | bytes 1540 | tf_op jit(solution)/shard_map/while
  587.7 201.6 %copy-start.67 = (f32[128]{0:T(128)}, f32[128]{0:T(128)S(1)}, u32[]{:S(2)}) copy-start(f32[128]{0:T(128)S(1)} %add_rsqrt_fusion.4) | copy-start | bytes 1540 | tf_op jit(solution)/shard_map/while
  627.6 79.7 %copy-start.79 = (bf16[8192]{0:T(1024)(128)(2,1)S(1)}, bf16[8192]{0:T(1024)(128)(2,1)}, u32[]{:S(2)}) copy-start(bf16[8192]{0:T(1024)(128)(2,1)} %get-tuple-element.1535) | copy-start | bytes 49156 | tf_op jit(solution)/shard_map/while
  628.4 181.8 %copy-start.31 = (bf16[128,512]{0,1:T(8,128)(2,1)}, bf16[128,512]{0,1:T(8,128)(2,1)S(1)}, u32[]{:S(2)}) copy-start(bf16[128,512]{0,1:T(8,128)(2,1)S(1)} %copy.81) | copy-start | bytes 393220 | tf_op jit(solution)/shard_map/while
  668.9 80.8 %copy-start.78 = (bf16[8192]{0:T(1024)(128)(2,1)S(1)}, bf16[8192]{0:T(1024)(128)(2,1)}, u32[]{:S(2)}) copy-start(bf16[8192]{0:T(1024)(128)(2,1)} %get-tuple-element.1534) | copy-start | bytes 49156 | tf_op jit(solution)/shard_map/while
  670.8 118.9 %copy-start.85 = (f32[128]{0:T(128)}, f32[128]{0:T(128)S(1)}, u32[]{:S(2)}) copy-start(f32[128]{0:T(128)S(1)} %get-tuple-element.1295) | copy-start | bytes 1540 | tf_op jit(solution)/shard_map/while
  672.8 315.1 %all-gather.29.cloned.1.call-start = ((), (), s32[]{:S(2)}) async-start(), calls=%async_computation.4 | async-start | bytes 8912896 | tf_op jit(solution)/shard_map/while/body/eval_jaxpr/all_gather | solution.py:22
  1073.4 265.0 %all-reduce.20.cloned.1.call-start = ((), (), s32[]{:S(2)}) async-start(), calls=%async_computation | async-start | bytes 27262976
  (173 other events, 1624.4 us)
Sparse Core Ops, SparseCore 0:
  12.3 59.5 all-gather.26
  75.2 55.6 all-gather.24
  142.7 75.0 all-gather.22
  385.5 72.0 all-gather.28
  547.0 55.2 all-gather.26
  605.3 55.7 all-gather.24
  672.9 74.6 all-gather.22
  915.4 72.4 all-gather.28
Sparse Core Ops, SparseCore 1:
  1090.8 247.5 all-reduce.19
where the time goes:
time: 1360 us
  blocking collectives  585 us (43%)
  waiting for transfers between devices  266 us (20%)
  other arithmetic  155 us (11%)
  loops' own time  132 us (10%)
  local copies, waits for them, and re-layouts  113 us (8%)
  matrix products  90.3 us (7%)
  between operations  15.6 us (1%)
    unnamed x2, waiting for transfers between devices  207 us
    all_gather x6, blocking collectives, carried_in(): everything = jax.tree.map(lambda part: lax.all_gather(part, axis), array)  142 us
    select_n x128, other arithmetic, step(): return jax.tree.map(lambda a, b: jnp.where(reached, a, b), new, before)  132 us
    another operation x4, loops' own time, carried_in(): return lax.fori_loop(0, peers, step, start)  127 us
    all_gather x2, blocking collectives, micro_step(): lax.all_gather(w_value, ('dp', 'seq'), axis=0, tiled=True)  85.9 us
    all_gather x2, blocking collectives, micro_step(): lax.all_gather(w_out, ('dp', 'seq'), axis=0, tiled=True)  80.5 us
    all_gather x2, blocking collectives, micro_step(): lax.all_gather(w_control, ('dp', 'seq'), axis=0, tiled=True)  80.2 us
    all_gather x2, blocking collectives, micro_step(): lax.all_gather(w_query, ('dp', 'seq'), axis=0, tiled=True)  78.2 us
  transfers between devices with their start and end apart: 9, of which 3 were waited for; matrix products, arithmetic and copies ran while one was open for 6% of the time, Pallas kernels for 0%

commit v1 on v0

v1 whole, which is shorter than its diff:
```python
import functools

import jax
import jax.numpy as jnp
from jax import lax
from jax.experimental import pallas as pl
from jax.experimental.pallas import tpu as pltpu
from jax.sharding import PartitionSpec as P

D = 512
FF = 2048
TOK = 128
SEQB = 2
OUTER = 4
BF = jnp.bfloat16
F32 = jnp.float32
EPS = 1e-05
MESH = pl.DeviceIdType.MESH
AXES = "aoic"


def nn(a, b):
    return jnp.dot(a, b, preferred_element_type=F32)


def nt(a, b):
    return lax.dot_general(a, b, (((1,), (1,)), ((), ())), preferred_element_type=F32)


def tn(a, b):
    return lax.dot_general(a, b, (((0,), (0,)), ((), ())), preferred_element_type=F32)


def halves(v):
    high = v.astype(BF)
    return high, (v - high.astype(F32)).astype(BF)


def norm_rows(v):
    center = v - jnp.mean(v, axis=-1, keepdims=True)
    inv = lax.rsqrt(jnp.mean(center * center, axis=-1, keepdims=True) + EPS)
    return center * inv, inv


def norm_back(g, unit, inv):
    return inv * (
        g - jnp.mean(g, axis=-1, keepdims=True) - unit * jnp.mean(g * unit, axis=-1, keepdims=True)
    )


def layout(na, ni):
    nch = OUTER * ni
    rows = 512 // nch
    lead = (na, OUTER, ni, 2)
    s = {}

    def vm(name, shape, dtype):
        s[name] = pltpu.VMEM(tuple(shape), dtype)

    vm("tmp", (256, 128), F32)
    vm("agq", lead + (16, 1024), BF)
    vm("sendq", (16, 1024), BF)
    vm("ago", lead + (16, 512), BF)
    vm("agu", lead + (16, FF), BF)
    vm("agd", lead + (64, 512), BF)
    vm("unit1", (256, 512), F32)
    vm("inv1", (256, 128), F32)
    vm("norm1", (SEQB, 2, TOK, 512), BF)
    vm("mini", (2, 8, 128), F32)
    for m in ("mask", "maskt"):
        vm(m, (SEQB, 256, 256), F32)
    for m in ("last", "use", "padb"):
        vm(m, (SEQB, 256, 128), F32)
    for m in ("q", "k", "v", "whi", "wlo"):
        vm(m, (4, 256, 128), BF)
    for m in ("w", "num", "tot", "share", "score", "dtot", "dkl", "dvl", "dwl"):
        vm(m, (4, 256, 128), F32)
    vm("dnum", (4, 256, 128), BF)
    vm("info", (8, 128), F32)
    for m in ("sloc", "rcv", "dloc", "drcv"):
        vm(m, (nch, rows + 8, 128), F32)
    for m in ("snd", "stin", "dsnd", "gin"):
        vm(m, (nch, rows, 128), F32)
    vm("zin", (8, 128), F32)
    vm("gz", (8, 128), F32)
    vm("outb", (4, 2, TOK, 128), BF)
    vm("mixx", (2, 4, TOK, 128), BF)
    vm("mixed", (256, 512), BF)
    for m in ("res", "unit2", "yacc", "dn2", "dres"):
        vm(m, (256, 512), F32)
    vm("inv2", (256, 128), F32)
    vm("n2", (256, 512), BF)
    vm("do", (4, 2, TOK, 128), BF)
    vm("senddo", (4, TOK, 128), BF)
    vm("dd", (SEQB, 2, TOK, 1024), BF)
    vm("dn1", (2, SEQB, TOK, 512), F32)
    vm("dn1r", (SEQB, TOK, 512), F32)
    vm("gq", lead + (16, 1024), BF)
    vm("go", lead + (16, 512), BF)
    vm("gu", lead + (16, FF), BF)
    vm("gd", lead + (64, 512), BF)
    vm("final", (2, 16, 1024), F32)
    vm("fsend", (16, 1024), F32)
    for ax, size in (("c", 2), ("i", ni), ("a", na), ("o", OUTER)):
        vm("gain_" + ax, (size, 8, 512), F32)
    for name, _, order, width, height in pieces(na, ni):
        dims = list(AXES)
        for step, ax in enumerate(order):
            size = dict(a=na, o=OUTER, i=ni, c=2)
            dims.remove(ax)
            left = tuple(size[d] for d in dims)
            vm(f"r{name}{step}", (max(size[ax] - 1, 1),) + left + (height, width), BF)
            if step < len(order) - 1:
                vm(f"s{name}{step}", left + (height, width), BF)
    s["sems"] = pltpu.SemaphoreType.DMA((2 * 200,))
    return s


def pieces(na, ni):
    return (
        ("q", "gq", "iao", 256, 16),
        ("k", "gq", "aio", 256, 16),
        ("v", "gq", "iao", 256, 16),
        ("x", "gq", "aio", 256, 16),
        ("o", "go", "ciao", 512, 16),
        ("u0", "gu", "ciao", 1024, 16),
        ("u1", "gu", "caio", 1024, 16),
        ("d0", "gd", "ciao", 256, 64),
        ("d1", "gd", "caio", 256, 64),
    )


def kernel(na, ni, names, *refs):
    (x_ref, dy_ref, seg_ref, pad_ref, wq_ref, wk_ref, wv_ref, wc_ref, wo_ref, wu_ref, wd_ref) = refs[:11]
    ga_ref, gf_ref = refs[11:13]
    (y_ref, dx_ref, oq_ref, ok_ref, ov_ref, oc_ref, oo_ref, ou_ref, od_ref, og1_ref, og2_ref) = refs[13:24]
    r = dict(zip(names, refs[24:], strict=True))
    nch = OUTER * ni
    rows = 512 // nch
    per = 64 // rows

    dp = lax.axis_index("dp")
    seq = lax.axis_index("seq")
    chip = seq // 2
    at = dict(a=dp if na > 1 else 0, o=chip // ni, i=lax.rem(chip, ni), c=lax.rem(seq, 2))
    size = dict(a=na, o=OUTER, i=ni, c=2)
    core = at["c"]

    def device(**moved):
        p = {**at, **moved}
        return (p["a"] if na > 1 else dp, (p["o"] * ni + p["i"]) * 2 + p["c"])

    def chip_device(t):
        return (dp, t * 2 + core)

    started = []
    sems = r["sems"]

    def remote(src, dst, dev):
        n = len(started)
        copy = pltpu.make_async_remote_copy(
            src_ref=src,
            dst_ref=dst,
            send_sem=sems.at[2 * n],
            recv_sem=sems.at[2 * n + 1],
            device_id=dev,
            device_id_type=MESH,
        )
        copy.start()
        started.append(copy)
        return copy

    def arrived(copies):
        for copy in copies:
            copy.wait_recv()

    mate = device(c=1 - core)

    barrier = pltpu.get_barrier_semaphore()
    greet = [mate] + [chip_device(lax.rem(chip + k, nch)) for k in range(1, nch)]
    greet += [device(a=lax.rem(at["a"] + k, na)) for k in range(1, na)]
    for dev in greet:
        pl.semaphore_signal(barrier, inc=1, device_id=dev, device_id_type=MESH)

    lane = lax.broadcasted_iota(jnp.int32, (1, 128), 1)
    low = (lane < 64).astype(F32)
    high = 1.0 - low
    lowb, highb = low.astype(BF), high.astype(BF)
    hm = (lowb, highb)
    first_core = core == 0

    tmp = r["tmp"]

    def unpack(ref, height, width):
        lines = height * width // 128
        tmp[0:lines, :] = ref[...].astype(F32)
        step = width // 128
        return [tmp[pl.ds(j, height, stride=step), :].astype(BF) for j in range(step)]

    own = (at["a"], at["o"], at["i"], core)
    agq, ago, agu, agd = r["agq"], r["ago"], r["agu"], r["agd"]
    for w, ref in enumerate((wq_ref, wk_ref, wv_ref, wc_ref)):
        blk = unpack(ref, 16, 512)
        for j in range(2):
            cols = slice(w * 256 + j * 128, w * 256 + j * 128 + 128)
            agq[own + (slice(None), cols)] = jnp.where(first_core, blk[j], blk[2 + j])
            r["sendq"][:, cols] = jnp.where(first_core, blk[2 + j], blk[j])
    for ref, buf, height, width in ((wo_ref, ago, 16, 512), (wu_ref, agu, 16, FF), (wd_ref, agd, 64, 512)):
        for j, blk in enumerate(unpack(ref, height, width)):
            buf[own + (slice(None), slice(j * 128, j * 128 + 128))] = blk

    x = x_ref[...].reshape(256, 512).astype(F32)
    unit, inv = norm_rows(x)
    r["unit1"][...] = unit
    r["inv1"][...] = jnp.broadcast_to(inv, (256, 128))
    n1own = (unit * ga_ref[...]).astype(BF)
    norm1 = r["norm1"]
    for b in range(SEQB):
        norm1[b, core] = n1own[b * TOK : (b + 1) * TOK]
    mini = r["mini"]
    mini[core, 0:2, :] = seg_ref[...].astype(F32)
    mini[core, 2:4, :] = pad_ref[...].astype(F32)
    mini[core, 4:8, :] = jnp.zeros((4, 128), F32)

    pl.semaphore_wait(barrier, len(greet))

    swap_w = remote(r["sendq"], agq.at[own], mate)
    swap_m = remote(mini.at[core], mini.at[core], mate)
    swap_n = remote(norm1.at[:, core], norm1.at[:, core], mate)

    def gather(buf, axis, done, lo, width):
        cols = pl.ds(lo, width)
        index = tuple(slice(None) if d in done else pl.ds(at[d], 1) for d in AXES)
        ref = buf.at[index + (slice(None), cols)]
        return [
            remote(ref, ref, device(**{axis: lax.rem(at[axis] + k, size[axis])}))
            for k in range(1, size[axis])
        ]

    swap_w.wait_recv()
    first = ((768, "ia"), (256, "ai"), (512, "ia"), (0, "ai"))
    rest = (
        (ago, 0, 512, "ia"),
        (agu, 0, 1024, "ai"),
        (agu, 1024, 1024, "ia"),
        (agd, 0, 256, "ai"),
        (agd, 256, 256, "ia"),
    )
    step_o = [gather(agq, "o", "c", lo, 256) for lo, _ in first]
    step_1, step_2 = [], []
    for (lo, order), got in zip(first, step_o):
        arrived(got)
        step_1.append(gather(agq, order[0], "co", lo, 256))
    rest_o = [gather(buf, "o", "", lo, width) for buf, lo, width, _ in rest]

    arrived([swap_m, swap_n])
    turned = [mini[s].T for s in range(2)]
    big_row = lax.broadcasted_iota(jnp.int32, (256, 256), 0)
    big_col = lax.broadcasted_iota(jnp.int32, (256, 256), 1)
    for b in range(SEQB):
        seg_row = jnp.concatenate([mini[0, b : b + 1, :], mini[1, b : b + 1, :]], axis=1)
        seg_col = jnp.concatenate([t[:, b : b + 1] for t in turned], axis=0)
        pad_col = jnp.concatenate([t[:, 2 + b : 3 + b] for t in turned], axis=0)
        same = seg_col == seg_row
        r["mask"][b] = jnp.where(same & (big_row >= big_col), 1.0, 0.0)
        r["maskt"][b] = jnp.where(same & (big_row <= big_col), 1.0, 0.0)
        seg_last = seg_row[:, 255:256]
        r["last"][b] = jnp.broadcast_to((seg_col == seg_last).astype(F32), (256, 128))
        r["padb"][b] = jnp.broadcast_to(pad_col, (256, 128))
        r["info"][4 + b : 5 + b, :] = jnp.broadcast_to(seg_last, (1, 128))
        r["info"][6 + b : 7 + b, :] = jnp.broadcast_to(seg_row[:, 0:1], (1, 128))

    for (lo, order), got in zip(first, step_1):
        arrived(got)
        step_2.append(gather(agq, order[1], "co" + order[0], lo, 256))

    def project(w):
        arrived(step_2[{3: 0, 1: 1, 2: 2, 0: 3}[w]])
        mat = agq[..., w * 256 : w * 256 + 256].reshape(512, 256)
        for b in range(SEQB):
            out = nn(norm1[b].reshape(256, 512), mat)
            for pair in range(2):
                part = out[:, pair * 128 : pair * 128 + 128]
                n = b * 2 + pair
                if w == 3:
                    weight = jnp.exp(part) * r["padb"][b]
                    r["w"][n] = weight
                    r["whi"][n], r["wlo"][n] = halves(weight)
                else:
                    r[("q", "k", "v")[w]][n] = part.astype(BF)

    for w in (3, 1, 2):
        project(w)

    def fold(full):
        return full[0:64] * low + full[64:128] * high

    def put_state(ref, n, which, value):
        for t in range(per):
            ref[(n * 2 + which) * per + t, 0:rows, :] = value[t * rows : (t + 1) * rows]

    def get_block(ref, n, which):
        value = ref[pl.ds((n * 2 + which) * per, per)].reshape(64, 128)
        return jnp.concatenate([value * low, value * high], axis=0)

    def local_state(n, carry):
        weight = r["w"][n] * r["last"][n // 2]
        hi, lo = halves(weight)
        for which, name in ((0, "k"), (1, "v")):
            rhs = r[name][n]
            put_state(r["sloc"], n, which, fold(tn(hi, rhs) + tn(lo, rhs)))
        r["info"][pl.ds(n, 1), :] = jnp.sum(weight, axis=0, keepdims=True)
        return carry

    lax.fori_loop(0, 4, local_state, 0)

    def spread(src, dst, info):
        for t in range(nch):
            src[t, rows : rows + 8, :] = info
        dst[chip] = src[chip]
        return [
            remote(src.at[lax.rem(chip + k, nch)], dst.at[chip], chip_device(lax.rem(chip + k, nch)))
            for k in range(1, nch)
        ]

    def back(src, dst):
        dst[chip] = src[chip]
        return [
            remote(src.at[lax.rem(chip + k, nch)], dst.at[chip], chip_device(lax.rem(chip + k, nch)))
            for k in range(1, nch)
        ]

    out_1 = spread(r["sloc"], r["rcv"], r["info"][...])

    project(0)
    rest_1 = []
    for (buf, lo, width, order), got in zip(rest, rest_o):
        arrived(got)
        rest_1.append(gather(buf, order[0], "o", lo, width))

    def mix_local(n, carry):
        q, k, whi, wlo = r["q"][n], r["k"][n], r["whi"][n], r["wlo"][n]
        mask = r["mask"][n // 2]
        num = jnp.zeros((256, 128), F32)
        for m in hm:
            hi, lo = halves(nt(q * m, k) * mask)
            num += nn(hi, whi * m) + nn(lo, whi * m) + nn(hi, wlo * m)
        r["num"][n] = num
        maskb = mask.astype(BF)
        r["tot"][n] = nn(maskb, whi) + nn(maskb, wlo)
        return carry

    lax.fori_loop(0, 4, mix_local, 0)

    arrived(out_1)
    rcv = r["rcv"]
    owned = (chip * rows) // 256

    def last_of(p, b):
        return rcv[p, pl.ds(rows + 4 + b, 1), :]

    def first_of(p, b):
        return rcv[p, pl.ds(rows + 6 + b, 1), :]

    run = jnp.zeros((rows, 128), F32)
    for p in range(nch):
        r["snd"][p] = run
        if p == 0:
            run = rcv[0, 0:rows, :]
        else:
            keep = (last_of(p - 1, owned) == last_of(p, owned)).astype(F32)
            run = rcv[p, 0:rows, :] + keep * run
    out_2 = back(r["snd"], r["stin"])
    zrun = [jnp.zeros((2, 128), F32) for _ in range(SEQB)]
    for p in range(nch - 1):
        for b in range(SEQB):
            z = rcv[p, rows + 2 * b : rows + 2 * b + 2, :]
            if p > 0:
                z = z + (last_of(p - 1, b) == last_of(p, b)).astype(F32) * zrun[b]
            zrun[b] = jnp.where(p < chip, z, zrun[b])
    before = jnp.maximum(chip - 1, 0)
    for b in range(SEQB):
        r["zin"][2 * b : 2 * b + 2, :] = zrun[b]
        open_doc = jnp.where(chip > 0, last_of(before, b), -1.0)[:, 0:1]
        seg_col = jnp.concatenate([t[:, b : b + 1] for t in turned], axis=0)
        r["use"][b] = jnp.broadcast_to((seg_col == open_doc).astype(F32), (256, 128))

    rest_2 = []
    for (buf, lo, width, order), got in zip(rest, rest_1):
        arrived(got)
        rest_2.append(gather(buf, order[1], "o" + order[0], lo, width))

    arrived(out_2)

    def both(op, v):
        if op is jnp.max:
            a = jnp.max(jnp.where(lane < 64, v, -jnp.inf), axis=1, keepdims=True)
            b = jnp.max(jnp.where(lane < 64, -jnp.inf, v), axis=1, keepdims=True)
        else:
            a = jnp.sum(v * low, axis=1, keepdims=True)
            b = jnp.sum(v * high, axis=1, keepdims=True)
        return jnp.where(lane < 64, a, b)

    def mix_rest(n, carry):
        b = n // 2
        q, v, whi = r["q"][n], r["v"][n], r["whi"][n]
        mask, use = r["mask"][b], r["use"][b]
        khi, klo = halves(get_block(r["stin"], n, 0))
        num = r["num"][n] + use * (nt(q, khi) + nt(q, klo))
        tot = r["tot"][n] + use * r["zin"][pl.ds(n, 1), :]
        floor = jnp.maximum(tot, 1.0)
        score = num / (floor * 8.0)
        e = jnp.exp(score - both(jnp.max, score))
        share = e / (both(jnp.sum, e) * floor)
        r["tot"][n] = tot
        r["score"][n] = score
        r["share"][n] = share
        sb = share.astype(BF)
        out = use * nn(sb, get_block(r["stin"], n, 1).astype(BF))
        for m in hm:
            out += nn((nt(sb * m, whi) * mask).astype(BF), v * m)
        r["outb"][n] = out.astype(BF).reshape(2, TOK, 128)
        return carry

    lax.fori_loop(0, 4, mix_rest, 0)
    swap_o = remote(r["outb"].at[:, 1 - core], r["mixx"].at[core], mate)
    for n in range(4):
        r["mixx"][core, n] = r["outb"][n, core]

    rest_3 = []
    for (buf, lo, width, order), got in zip(rest, rest_2):
        arrived(got)
        rest_3.append(gather(buf, "c", "oai", lo, width))

    swap_o.wait_recv()
    arrived(rest_3[0])
    mixx = r["mixx"]
    for b in range(SEQB):
        r["mixed"][b * TOK : (b + 1) * TOK, :] = jnp.concatenate(
            [mixx[h, b * 2 + p] for h in range(2) for p in range(2)], axis=1
        )
    w_out = ago[...].reshape(512, 512)
    residual = x_ref[...].reshape(256, 512).astype(F32) + nn(r["mixed"][...], w_out)
    r["res"][...] = residual
    unit, inv = norm_rows(residual)
    r["unit2"][...] = unit
    r["inv2"][...] = jnp.broadcast_to(inv, (256, 128))
    r["n2"][...] = (unit * gf_ref[...]).astype(BF)
    for copies in rest_3[1:]:
        arrived(copies)

    r["yacc"][...] = jnp.zeros((256, 512), F32)
    r["dn2"][...] = jnp.zeros((256, 512), F32)
    span = na * OUTER // 4

    def feed(j, carry):
        dy = dy_ref[...].reshape(256, 512)
        n2 = r["n2"][...]
        cols = pl.ds(pl.multiple_of(j * 512, 512), 512)
        up = agu[:, :, :, :, :, cols].reshape(512, 512)
        place = (j * span // OUTER, pl.ds(lax.rem(j * span, OUTER), span))
        down = agd[place].reshape(512, 512)
        pre = nn(n2, up)
        sig = 1.0 / (1.0 + jnp.exp(-pre))
        hidden = (pre * sig).astype(BF)
        r["yacc"][...] += nn(hidden, down)
        d_pre = (nt(dy, down) * (sig * (1.0 + pre * (1.0 - sig)))).astype(BF)
        r["dn2"][...] += nt(d_pre, up)
        r["gd"][place] = tn(hidden, dy).astype(BF).reshape((span, ni, 2, 64, 512))
        r["gu"][:, :, :, :, :, cols] = tn(n2, d_pre).astype(BF).reshape((na, OUTER, ni, 2, 16, 512))
        return carry

    lax.fori_loop(0, 4, feed, 0)

    class Sum:
        def __init__(self, name, buffer, order, width, height, lo):
            self.name, self.order, self.width, self.height = name, order, width, height
            self.ref, self.lo, self.dims, self.step = r[buffer], lo, list(AXES), 0

        def start(self):
            ax = self.order[self.step]
            p = self.dims.index(ax)
            cols = pl.ds(self.lo, self.width)
            land = r[f"r{self.name}{self.step}"]
            self.copies = []
            for k in range(1, size[ax]):
                to = lax.rem(at[ax] + k, size[ax])
                index = [slice(None)] * len(self.dims) + [slice(None), cols]
                index[p] = to
                self.copies.append(remote(self.ref.at[tuple(index)], land.at[k - 1], device(**{ax: to})))

        def finish(self, emit=None):
            ax = self.order[self.step]
            p = self.dims.index(ax)
            arrived(self.copies)
            land = r[f"r{self.name}{self.step}"]
            cols = slice(self.lo, self.lo + self.width)
            left = [size[d] for d in self.dims if d != ax]
            total = 1
            for extent in left:
                total *= extent
            into = None if emit else r[f"s{self.name}{self.step}"]

            def one(flat):
                index, rest_of = [], flat
                for extent in reversed(left):
                    index.insert(0, rest_of % extent if isinstance(rest_of, int) else lax.rem(rest_of, extent))
                    rest_of = rest_of // extent
                full = list(index)
                full.insert(p, at[ax])
                value = self.ref[tuple(full) + (slice(None), cols)].astype(F32)
                for k in range(size[ax] - 1):
                    value += land[(k,) + tuple(index)].astype(F32)
                if emit:
                    emit(index, value)
                else:
                    into[tuple(index)] = value.astype(BF)

            if total <= 2:
                for flat in range(total):
                    one(flat)
            else:
                def body(flat, carry):
                    one(flat)
                    return carry

                lax.fori_loop(0, total, body, 0)
            self.dims.remove(ax)
            self.ref, self.lo, self.step = into, 0, self.step + 1

    specs = {name: (name, buf, order, width, height) for name, buf, order, width, height in pieces(na, ni)}
    place = dict(q=0, k=256, v=512, x=768, o=0, u0=0, u1=1024, d0=0, d1=256)
    sums = {name: Sum(*spec, place[name]) for name, spec in specs.items()}
    ffn = [sums[n] for n in ("d0", "d1", "u0", "u1")]
    for s in ffn:
        s.start()

    y_ref[...] = (r["res"][...] + r["yacc"][...]).astype(BF).reshape(SEQB, TOK, 512)
    dn2 = r["dn2"][...]
    unit = r["unit2"][...]
    gains2 = jnp.sum(dn2 * unit, axis=0, keepdims=True)
    d_res = dy_ref[...].reshape(256, 512).astype(F32) + norm_back(
        dn2 * gf_ref[...], unit, r["inv2"][:, 0:1]
    )
    r["dres"][...] = d_res
    d_attn = d_res.astype(BF)
    d_mixed = nt(d_attn, w_out).astype(BF)
    for b in range(SEQB):
        for p in range(2):
            part = [d_mixed[b * TOK : (b + 1) * TOK, h * 256 + p * 128 : h * 256 + p * 128 + 128] for h in range(2)]
            r["do"][b * 2 + p, core] = jnp.where(first_core, part[0], part[1])
            r["senddo"][b * 2 + p] = jnp.where(first_core, part[1], part[0])
    swap_d = remote(r["senddo"], r["do"].at[:, core], mate)
    r["go"][...] = tn(r["mixed"][...], d_attn).astype(BF).reshape((na, OUTER, ni, 2, 16, 512))
    sums["o"].start()
    for s in ffn:
        s.finish()
        s.start()
    sums["o"].finish()
    sums["o"].start()
    swap_d.wait_recv()

    def mix_back(n, carry):
        b = n // 2
        q, v, whi = r["q"][n], r["v"][n], r["whi"][n]
        mask, use = r["mask"][b], r["use"][b]
        share, tot, score = r["share"][n], r["tot"][n], r["score"][n]
        d_out = r["do"][n].reshape(256, 128)
        ds = use * nt(d_out, get_block(r["stin"], n, 1).astype(BF))
        for m in hm:
            ds += nn((nt(d_out * m, v) * mask).astype(BF), whi * m)
        floor = jnp.maximum(tot, 1.0)
        inv_floor = 1.0 / floor
        prob = share * floor
        dprob = ds * inv_floor
        dscore = prob * (dprob - both(jnp.sum, dprob * prob))
        dnum = dscore * inv_floor * 0.125
        gate = jnp.where(tot > 1.0, 1.0, jnp.where(tot == 1.0, 0.5, 0.0))
        dtot = -(ds * share + dscore * score) * inv_floor * gate
        r["dnum"][n] = dnum.astype(BF)
        r["dtot"][n] = dtot
        put_state(r["dloc"], n, 0, fold(tn((use * dnum).astype(BF), q)))
        put_state(r["dloc"], n, 1, fold(tn((use * share).astype(BF), d_out)))
        r["gz"][pl.ds(n, 1), :] = jnp.sum(use * dtot, axis=0, keepdims=True)
        return carry

    lax.fori_loop(0, 4, mix_back, 0)
    r["gz"][4:8, :] = jnp.zeros((4, 128), F32)
    out_3 = spread(r["dloc"], r["drcv"], r["gz"][...])

    def mix_back_local(n, carry):
        b = n // 2
        q, k, v, whi, w = r["q"][n], r["k"][n], r["v"][n], r["whi"][n], r["w"][n]
        mask, maskt, use = r["mask"][b], r["maskt"][b], r["use"][b]
        d_out, dnum = r["do"][n].reshape(256, 128), r["dnum"][n]
        sb = r["share"][n].astype(BF)
        dq = use * nn(dnum, get_block(r["stin"], n, 0).astype(BF))
        dk = jnp.zeros((256, 128), F32)
        dv = jnp.zeros((256, 128), F32)
        dw = nn(maskt.astype(BF), r["dtot"][n].astype(BF))
        for m in hm:
            dq += nn((nt(dnum * m, whi) * mask).astype(BF), k * m)
            dk += nn((nt(whi * m, dnum) * maskt).astype(BF), q * m)
            dv += nn((nt(whi * m, sb) * maskt).astype(BF), d_out * m)
            dw += nn((nt(v * m, d_out) * maskt).astype(BF), sb * m)
            dw += nn((nt(k * m, q) * maskt).astype(BF), dnum * m)
        cols = pl.ds(pl.multiple_of(lax.rem(n, 2) * 128, 128), 128)
        r["dd"][b, :, :, cols] = dq.astype(BF).reshape(2, TOK, 128)
        r["dkl"][n] = dk
        r["dvl"][n] = dv
        r["dwl"][n] = dw
        return carry

    lax.fori_loop(0, 4, mix_back_local, 0)
    dd = r["dd"]

    def weight_gradient(lo, width):
        left = norm1[...].reshape(512, 512)
        value = tn(left, dd[:, :, :, lo : lo + width].reshape(512, width))
        r["gq"][:, :, :, :, :, lo : lo + width] = value.astype(BF).reshape((na, OUTER, ni, 2, 16, width))

    weight_gradient(0, 256)
    sums["q"].start()
    for s in ffn:
        s.finish()
        s.start()
    sums["o"].finish()
    sums["o"].start()

    arrived(out_3)
    drcv = r["drcv"]
    run = jnp.zeros((rows, 128), F32)
    for p in reversed(range(nch)):
        r["dsnd"][p] = run
        if p == nch - 1:
            run = drcv[p, 0:rows, :]
        else:
            keep = (first_of(p, owned) == first_of(p + 1, owned)).astype(F32)
            run = drcv[p, 0:rows, :] + keep * run
    out_4 = back(r["dsnd"], r["gin"])
    zrun = [jnp.zeros((2, 128), F32) for _ in range(SEQB)]
    for p in reversed(range(1, nch)):
        for b in range(SEQB):
            z = drcv[p, rows + 2 * b - 0 : rows + 2 * b + 2, :]
            if p < nch - 1:
                z = z + (first_of(p, b) == first_of(p + 1, b)).astype(F32) * zrun[b]
            zrun[b] = jnp.where(p > chip, z, zrun[b])
    after = jnp.minimum(chip + 1, nch - 1)
    for b in range(SEQB):
        r["gz"][2 * b : 2 * b + 2, :] = zrun[b]
        matched = (first_of(after, b) == r["info"][4 + b : 5 + b, :]) & (chip < nch - 1)
        r["last"][b] = r["last"][b] * matched.astype(F32)
    sums["q"].finish()
    sums["q"].start()
    arrived(out_4)

    def mix_last(n, carry):
        b = n // 2
        k, v, whi, w, last = r["k"][n], r["v"][n], r["whi"][n], r["w"][n], r["last"][b]
        gk = get_block(r["gin"], n, 0).astype(BF)
        gv = get_block(r["gin"], n, 1).astype(BF)
        dk = r["dkl"][n] + last * nn(whi, gk)
        dv = r["dvl"][n] + last * nn(whi, gv)
        dw = r["dwl"][n] + last * (nt(k, gk) + nt(v, gv) + r["gz"][pl.ds(n, 1), :])
        for slot, value in ((1, dk), (2, dv), (3, dw * w)):
            cols = pl.ds(pl.multiple_of(slot * 256 + lax.rem(n, 2) * 128, 128), 128)
            dd[b, :, :, cols] = value.astype(BF).reshape(2, TOK, 128)
        return carry

    lax.fori_loop(0, 4, mix_last, 0)
    tail = [sums[n] for n in ("k", "v", "x")]
    for s, lo in zip(tail, (256, 512, 768)):
        weight_gradient(lo, 256)
        s.start()

    full_q = agq[...].reshape(512, 1024)
    for b in range(SEQB):
        part = nt(dd[b].reshape(256, 1024), full_q)
        r["dn1"][:, b] = part.reshape(2, TOK, 512)
    swap_g = remote(r["dn1"].at[1 - core], r["dn1r"], mate)

    def to_rows(out_ref, height, width):
        def emit(index, value, lo=0):
            step = width // 128
            for j in range(value.shape[1] // 128):
                out_ref[pl.ds(lo // 128 + j, height, stride=step), :] = value[:, j * 128 : j * 128 + 128]

        return emit

    ends = dict(
        o=(oo_ref, 16, 512, 0), u0=(ou_ref, 16, FF, 0), u1=(ou_ref, 16, FF, 1024), d0=(od_ref, 64, 512, 0), d1=(od_ref, 64, 512, 256)
    )
    for s in ffn + [sums["o"]]:
        s.finish()
        s.start()
    for s in tail + [sums["q"]]:
        s.finish()
        s.start()
    swap_g.wait_recv()
    dn1 = (r["dn1"][core] + r["dn1r"][...]).reshape(256, 512)
    unit = r["unit1"][...]
    gains1 = jnp.sum(dn1 * unit, axis=0, keepdims=True)
    dx = r["dres"][...] + norm_back(dn1 * ga_ref[...], unit, r["inv1"][:, 0:1])
    dx_ref[...] = dx.astype(BF).reshape(SEQB, TOK, 512)

    gains = jnp.concatenate([gains1, gains2, jnp.zeros((6, 512), F32)], axis=0)

    def gain_start(ax, value):
        buf = r["gain_" + ax]
        buf[at[ax]] = value
        return [
            remote(buf.at[at[ax]], buf.at[at[ax]], device(**{ax: lax.rem(at[ax] + k, size[ax])}))
            for k in range(1, size[ax])
        ]

    def gain_finish(ax, copies):
        arrived(copies)
        buf = r["gain_" + ax]
        value = buf[0]
        for k in range(1, size[ax]):
            value = value + buf[k]
        return value

    copies = gain_start("c", gains)
    gains = gain_finish("c", copies)
    copies = gain_start("i", gains)

    for s in ffn + [sums["o"]]:
        ref, height, width, lo = ends[s.name]
        s.finish(functools.partial(to_rows(ref, height, width), lo=lo))
    gains = gain_finish("i", copies)
    copies = gain_start("a", gains)
    for s in tail:
        s.finish()
        s.start()
    gains = gain_finish("a", copies)
    copies = gain_start("o", gains)

    final, fsend = r["final"], r["fsend"]
    home = dict(q=0, k=256, v=512, x=768)
    shards = {}
    for s in [sums["q"]] + tail:
        lo = home[s.name]
        got = {}

        def keep_value(index, value, got=got):
            got[index[0]] = value

        s.finish(keep_value)
        final[core, :, lo : lo + 256] = jnp.where(first_core, got[0], got[1])
        fsend[:, lo : lo + 256] = jnp.where(first_core, got[1], got[0])
    swap_f = remote(fsend, final.at[core], mate)
    gains = gain_finish("o", copies)
    og1_ref[...] = gains[0:1]
    og2_ref[...] = gains[1:2]
    swap_f.wait_recv()
    for ref, lo in ((oq_ref, 0), (ok_ref, 256), (ov_ref, 512), (oc_ref, 768)):
        for j in range(4):
            ref[pl.ds(j, 16, stride=4), :] = final[j // 2, :, lo + (j % 2) * 128 : lo + (j % 2) * 128 + 128]
    for copy in started:
        copy.wait_send()


def solution(mesh):
    ndp, nseq = mesh.shape["dp"], mesh.shape["seq"]
    joint = D // (ndp * nseq) >= 16
    na = ndp if joint else 1
    ni = nseq // (2 * OUTER)
    scratch = layout(na, ni)
    names = tuple(scratch)
    both_axes = ("dp", "seq")

    def body(x, dy, seg, pad, *args):
        weights, (gain_attn, gain_ffn) = args[:7], args[7:]
        shards = []
        for w in weights:
            if not joint:
                whole = lax.all_gather(w, both_axes, axis=0, tiled=True).reshape(nseq, -1)
                w = lax.dynamic_index_in_dim(whole, lax.axis_index("seq"), 0, keepdims=False)
            shards.append(w.reshape(-1, 128))
        outs = [jax.ShapeDtypeStruct(x.shape, BF)] * 2
        outs += [jax.ShapeDtypeStruct(w.shape, F32) for w in shards]
        outs += [jax.ShapeDtypeStruct((1, D), F32)] * 2
        vmem = pl.BlockSpec(memory_space=pltpu.VMEM)
        got = pl.pallas_call(
            functools.partial(kernel, na, ni, names),
            out_shape=outs,
            in_specs=[vmem] * 13,
            out_specs=[vmem] * 11,
            scratch_shapes=list(scratch.values()),
            compiler_params=pltpu.CompilerParams(
                collective_id=0, has_side_effects=True, vmem_limit_bytes=62 * 2**20
            ),
            cost_estimate=pl.CostEstimate(flops=12 * 10**9, bytes_accessed=4 * 2**20, transcendentals=10**6),
            name="block",
        )(x, dy, seg, pad, *shards, gain_attn.reshape(1, D), gain_ffn.reshape(1, D))
        y, dx = got[:2]
        grads = [g.reshape(-1) for g in got[2:9]]
        gains = [g.reshape(-1) for g in got[9:]]
        if not joint:
            index = lax.axis_index("dp") * nseq + lax.axis_index("seq")
            grads = [lax.psum(g, "dp") for g in grads]
            grads = [lax.all_gather(g, "seq", axis=0, tiled=True) for g in grads]
            grads = [
                lax.dynamic_slice_in_dim(g, index * (g.shape[0] // (ndp * nseq)), g.shape[0] // (ndp * nseq))
                for g in grads
            ]
            gains = [lax.psum(g, "dp") for g in gains]
        return (y, dx, *grads, *gains)

    data, ids, flat = P("dp", "seq", None), P("dp", "seq"), P(("dp", "seq"))
    return jax.shard_map(
        body,
        mesh=mesh,
        in_specs=(data, data, ids, ids) + (flat,) * 7 + (P(), P()),
        out_specs=(data, data) + (flat,) * 7 + (P(), P()),
        check_vma=False,
    )
```

time: 1360 us -> 133 us (0.10)
  blocking collectives: 585 us -> 0 us
  waiting for transfers between devices: 266 us -> 0 us
  other arithmetic: 155 us -> 0 us
  loops' own time: 132 us -> 0 us
  Pallas kernels: 0 us -> 123 us
  local copies, waits for them, and re-layouts: 113 us -> 8.6 us
  matrix products: 90.3 us -> 0 us
  between operations: 15.6 us -> 0.68 us
    all_gather x16 -> x0, blocking collectives: 544 us -> none  [the longest x6 142 us: carried_in(): everything = jax.tree.map(lambda part: lax.all_gather(part, axis), array)]
    unnamed x2 -> x0, waiting for transfers between devices: 207 us -> none
    select_n x132 -> x0, other arithmetic: 132 us -> none  [the longest x128 132 us: step(): return jax.tree.map(lambda a, b: jnp.where(reached, a, b), new, before)]
    another operation x5 -> x0, loops' own time: 132 us -> none  [the longest x4 127 us: carried_in(): return lax.fori_loop(0, peers, step, start)]
    pallas_call x0 -> x1, Pallas kernels: none -> 123 us  [body(): pl.pallas_call(functools.partial(kernel, na, ni, names), out_shape=outs,...]
    dot_general x90 -> x0, matrix products: 85.6 us -> none  [the longest x14 15.7 us: outer_rows(): lax.dot_general(left, right, (((0,), (0,)), ((), ())), preferred_element_...]
    all_gather x8 -> x0, waiting for transfers between devices: 56.7 us -> none  [the longest x4 56.6 us: carried_in(): everything = jax.tree.map(lambda part: lax.all_gather(part, axis), array)]
    psum x1 -> x0, blocking collectives: 40.4 us -> none  [body(): gain_sums = lax.psum((totals[7], totals[8]), ('dp', 'seq'))]
  transfers between devices with their start and end apart: 9 -> 0, of which waited for: 3 -> 0; matrix products, arithmetic and copies ran while one was open for 6% -> 0% of each run, Pallas kernels for 0% -> 0%
where the time goes in v1:
time: 133 us
  Pallas kernels  123 us (92%)
  local copies, waits for them, and re-layouts  8.6 us (6%)
    pallas_call x1, Pallas kernels, body(): pl.pallas_call(functools.partial(kernel, na, ni, names), out_shape=outs,...  123 us
    unnamed x31, local copies, waits for them, and re-layouts  8.6 us

profile of v1, /device:TPU:0, one launch (start us, length us, event | category | flops | bytes accessed | tf_op | source)
XLA Modules:
  0.0 132.6 jit_solution(3375456083509165855)
XLA Ops:
  0.6 123.3 %block.1 = (bf16[2,128,512]{2,1,0:T(8,128)(2,1)}, bf16[2,128,512]{2,1,0:T(8,128)(2,1)}, f32[64,128]{1,0:T(8,128)}, f32[64,128]{1,0:T(8,128)}, f32[64,128]{1,0:T(...) custom-call(bf16[2,128,512]{2,1,0:T(8,128)(2,1)} %refs_0_.1, ...), custom_call_target="tpu_custom_call" | custom-call | flops 12000000000 | bytes 4194304 | tf_op jit(solution)/shard_map/block/pallas_call | solution.py:785
  123.9 0.0 copy-start
  123.9 1.7 %copy.35 = bf16[2,128,512]{2,1,0:T(8,128)(2,1)} copy(bf16[2,128,512]{2,1,0:T(8,128)(2,1)} %get-tuple-element.44) | data formatting | bytes 524288
  125.7 0.0 copy-done
  125.7 0.0 copy-start.7
  125.7 0.0 copy-start.6
  125.7 0.7 copy.36
  126.4 0.1 copy-done.7
  126.4 0.0 copy-start.5
  126.4 0.0 copy-start.4
  126.4 0.6 copy.37
  127.0 0.0 copy-done.6
  127.0 0.0 copy-start.2
  127.0 0.6 copy.38
  127.7 0.0 copy-done.5
  127.7 0.6 copy.39
  128.3 0.0 copy-done.4
  128.3 0.0 copy-start.3
  128.3 0.6 copy.40
  128.9 0.2 copy-done.3
  129.1 0.6 copy.41
  129.7 0.0 copy-done.2
  129.7 0.0 copy-start.1
  129.7 0.7 copy.42
  130.3 0.3 copy-done.1
  130.6 0.0 copy-start.9
  130.6 0.7 copy.43
  131.3 0.0 copy-done.9
  131.3 0.0 copy-start.8
  131.3 0.6 copy.44
  131.9 0.1 copy-done.8
  132.0 0.6 copy.45
Async XLA Ops:
  123.9 1.7 %copy-start = (bf16[2,128,512]{2,1,0:T(8,128)(2,1)S(1)}, bf16[2,128,512]{2,1,0:T(8,128)(2,1)}, u32[]{:S(2)}) copy-start(bf16[2,128,512]{2,1,0:T(8,128)(2,1)} %get-tuple-element.45) | copy-start | bytes 786436
  125.7 0.8 copy-start.7
  125.7 1.4 %copy-start.6 = (f32[64,128]{1,0:T(8,128)S(1)}, f32[64,128]{1,0:T(8,128)}, u32[]{:S(2)}) copy-start(f32[64,128]{1,0:T(8,128)} %get-tuple-element.25) | copy-start | bytes 98308
  126.4 1.2 copy-start.5
  126.4 1.9 %copy-start.4 = (f32[64,128]{1,0:T(8,128)S(1)}, f32[64,128]{1,0:T(8,128)}, u32[]{:S(2)}) copy-start(f32[64,128]{1,0:T(8,128)} %get-tuple-element.27) | copy-start | bytes 98308
  127.0 2.6 %copy-start.2 = (f32[256,128]{1,0:T(8,128)S(1)}, f32[256,128]{1,0:T(8,128)}, u32[]{:S(2)}) copy-start(f32[256,128]{1,0:T(8,128)} %get-tuple-element.29) | copy-start | bytes 393220
  128.3 0.8 copy-start.3
  129.7 1.0 copy-start.1
  130.6 0.7 copy-start.9
  131.3 0.7 copy-start.8

commit v2 on v1

v2 whole, which is shorter than its diff:
```python
import functools
import types

import jax
import jax.numpy as jnp
from jax import lax
from jax.experimental import pallas as pl
from jax.experimental.pallas import tpu as pltpu
from jax.sharding import PartitionSpec as P

D = 512
FF = 2048
TOK = 128
SEQB = 2
OUTER = 4
BF = jnp.bfloat16
F32 = jnp.float32
EPS = 1e-05
MESH = pl.DeviceIdType.MESH
AXES = "aoic"


GATHER = (
    ("agq", 768, 256, "oia"),
    ("agq", 256, 256, "oai"),
    ("agq", 512, 256, "oia"),
    ("agq", 0, 256, "oia"),
    ("ago", 0, 512, "oai"),
    ("agu", 0, 512, "ioa"),
    ("agu", 512, 512, "ioa"),
    ("agu", 1024, 512, "oai"),
    ("agu", 1536, 512, "aoi"),
    ("agd", 0, 128, "oia"),
    ("agd", 128, 128, "oai"),
    ("agd", 256, 128, "aio"),
    ("agd", 384, 128, "oia"),
)
PIECE = (
    ("gq", "aio", 0, 256, 16),
    ("gq", "iao", 256, 256, 16),
    ("gq", "aio", 512, 256, 16),
    ("gq", "aio", 768, 256, 16),
    ("go", "ciao", 0, 512, 16),
    ("gu", "ciao", 0, 512, 16),
    ("gu", "cioa", 512, 512, 16),
    ("gu", "caoi", 1024, 512, 16),
    ("gu", "caio", 1536, 512, 16),
    ("gd", "cioa", 0, 128, 64),
    ("gd", "caoi", 128, 128, 64),
    ("gd", "coia", 256, 128, 64),
    ("gd", "cioa", 384, 128, 64),
)
SCHEDULE = (
    (10, 11, 4, 8, 0, 1, 2, 5, 6, 10, 3, 0, 1, 4, 7, 2, 5, 0),
    (3, 12, 1, 2, 4, 6, 10, 9, 3, 8, 0),
    (1,),
    (),
    (2,),
    (),
    (),
    (5, 6, 12, 11, 3, 7),
    (10, 9),
    (),
    (),
    (),
    (5, 8, 12, 4),
    (6, 7, 6, 9, 4, 5, 11),
    (),
    (),
    (7, 8),
    (),
    (12,),
    (10, 9, 11),
    (7,),
    (11, 8, 12, 9),
    (),
    (24,),
    (22, 19, 23),
    (),
    (),
    (),
    (19, 24, 22, 23, 25),
    (),
    (21,),
    (),
    (20,),
    (25, 17, 19, 21, 18),
    (),
    (),
    (),
    (),
    (17, 20, 23),
    (13, 19, 21, 22),
    (),
    (),
    (14, 17),
    (20,),
    (16,),
    (13,),
    (25, 24, 15),
    (18,),
    (21, 14, 16),
    (17,),
    (24, 22, 23, 13, 15, 25),
    (18, 14, 16, 15, 21),
    (19, 25, 18, 14, 23, 20, 16, 24),
    (17, 15, 13, 22),
    (),
    (),
    (20, 18),
)


def nn(a, b):
    return jnp.dot(a, b, preferred_element_type=F32)


def nt(a, b):
    return lax.dot_general(a, b, (((1,), (1,)), ((), ())), preferred_element_type=F32)


def tn(a, b):
    return lax.dot_general(a, b, (((0,), (0,)), ((), ())), preferred_element_type=F32)


def halves(v):
    high = v.astype(BF)
    return high, (v - high.astype(F32)).astype(BF)


def norm_rows(v):
    center = v - jnp.mean(v, axis=-1, keepdims=True)
    inv = lax.rsqrt(jnp.mean(center * center, axis=-1, keepdims=True) + EPS)
    return center * inv, inv


def norm_back(g, unit, inv):
    return inv * (
        g - jnp.mean(g, axis=-1, keepdims=True) - unit * jnp.mean(g * unit, axis=-1, keepdims=True)
    )


def layout(na, ni):
    nch = OUTER * ni
    rows = 512 // nch
    lead = (na, OUTER, ni, 2)
    s = {}

    def vm(name, shape, dtype):
        s[name] = pltpu.VMEM(tuple(shape), dtype)

    vm("tmp", (256, 128), F32)
    vm("agq", lead + (16, 1024), BF)
    vm("sendq", (16, 1024), BF)
    vm("ago", lead + (16, 512), BF)
    vm("agu", lead + (16, FF), BF)
    vm("agd", lead + (64, 512), BF)
    vm("unit1", (256, 512), F32)
    vm("inv1", (256, 128), F32)
    vm("norm1", (SEQB, 2, TOK, 512), BF)
    vm("mini", (2, 8, 128), F32)
    for m in ("mask", "maskt"):
        vm(m, (SEQB, 256, 256), F32)
    for m in ("last", "use", "padb"):
        vm(m, (SEQB, 256, 128), F32)
    for m in ("q", "k", "v", "whi", "wlo"):
        vm(m, (4, 256, 128), BF)
    for m in ("w", "num", "tot", "share", "score", "dtot", "dkl", "dvl", "dwl"):
        vm(m, (4, 256, 128), F32)
    vm("dnum", (4, 256, 128), BF)
    vm("info", (8, 128), F32)
    for m, kind, extra in (("sloc", F32, 8), ("rcv", F32, 8), ("dloc", BF, 16), ("drcv", BF, 16)):
        vm(m, (nch, rows + extra, 128), kind)
    for m, kind in (("snd", F32), ("stin", F32), ("dsnd", BF), ("gin", BF)):
        vm(m, (nch, rows, 128), kind)
    vm("zin", (8, 128), F32)
    vm("gz", (8, 128), F32)
    vm("outb", (4, 2, TOK, 128), BF)
    vm("mixx", (2, 4, TOK, 128), BF)
    vm("mixed", (256, 512), BF)
    for m in ("res", "unit2", "dn2", "dres"):
        vm(m, (256, 512), F32)
    vm("inv2", (256, 128), F32)
    vm("n2", (256, 512), BF)
    vm("n2t", (512, 256), BF)
    vm("norm1t", (512, 512), BF)
    vm("hidden", (256, FF), BF)
    vm("dsilu", (256, FF), F32)
    vm("xv", (SEQB, TOK, 512), BF)
    vm("dyv", (SEQB, TOK, 512), BF)
    for name, lines in (("wq", 64), ("wk", 64), ("wv", 64), ("wc", 64), ("wo", 64), ("wu", 256), ("wd", 256)):
        vm(name, (lines, 128), BF)
    vm("do", (4, 2, TOK, 128), BF)
    vm("senddo", (4, TOK, 128), BF)
    vm("dd", (SEQB, 2, TOK, 1024), BF)
    vm("dn1", (2, SEQB, TOK, 512), F32)
    vm("dn1r", (SEQB, TOK, 512), F32)
    vm("gq", lead + (16, 1024), BF)
    vm("go", lead + (16, 512), BF)
    vm("gu", lead + (16, FF), BF)
    vm("gd", lead + (64, 512), BF)
    vm("final", (2, 16, 1024), F32)
    vm("fsend", (16, 1024), F32)
    for name, size in (("gain1", 2), ("gain2", nch), ("gain3", na)):
        vm(name, (size, 8, 128), F32)
    for name, (_, order, _, width, height) in enumerate(PIECE):
        dims = list(AXES)
        for step, ax in enumerate(order):
            size = dict(a=na, o=OUTER, i=ni, c=2)
            dims.remove(ax)
            left = tuple(size[d] for d in dims)
            vm(f"r{name}_{step}", (max(size[ax] - 1, 1),) + left + (height, width), BF)
            if step < len(order) - 1:
                vm(f"s{name}_{step}", left + (height, width), BF)
    s["load"] = pltpu.SemaphoreType.DMA((9,))
    s["sems"] = pltpu.SemaphoreType.DMA((2 * 200,))
    return s


def kernel(na, ni, names, *refs):
    (x_ref, dy_ref, seg_ref, pad_ref, wq_ref, wk_ref, wv_ref, wc_ref, wo_ref, wu_ref, wd_ref) = refs[:11]
    ga_ref, gf_ref = refs[11:13]
    (y_ref, dx_ref, oq_ref, ok_ref, ov_ref, oc_ref, oo_ref, ou_ref, od_ref, og1_ref, og2_ref) = refs[13:24]
    r = types.SimpleNamespace(**dict(zip(names, refs[24:], strict=True)))
    nch = OUTER * ni
    rows = 512 // nch
    per = 64 // rows

    dp = lax.axis_index("dp")
    seq = lax.axis_index("seq")
    chip = seq // 2
    at = dict(a=dp if na > 1 else 0, o=chip // ni, i=lax.rem(chip, ni), c=lax.rem(seq, 2))
    size = dict(a=na, o=OUTER, i=ni, c=2)
    core = at["c"]

    def device(**moved):
        p = {**at, **moved}
        return (p["a"] if na > 1 else dp, (p["o"] * ni + p["i"]) * 2 + p["c"])

    def chip_device(t):
        return (dp, t * 2 + core)

    started = []
    sems = r.sems

    def remote(src, dst, dev):
        n = len(started)
        copy = pltpu.make_async_remote_copy(
            src_ref=src,
            dst_ref=dst,
            send_sem=sems.at[2 * n],
            recv_sem=sems.at[2 * n + 1],
            device_id=dev,
            device_id_type=MESH,
        )
        copy.start()
        started.append(copy)
        return copy

    def arrived(copies):
        for copy in copies:
            copy.wait_recv()

    mate = device(c=1 - core)

    barrier = pltpu.get_barrier_semaphore()
    greet = [mate] + [chip_device(lax.rem(chip + k, nch)) for k in range(1, nch)]
    greet += [device(a=lax.rem(at["a"] + k, na)) for k in range(1, na)]
    for dev in greet:
        pl.semaphore_signal(barrier, inc=1, device_id=dev, device_id_type=MESH)

    load = {}
    for name, ref in (
        ("wq", wq_ref), ("wk", wk_ref), ("wv", wv_ref), ("wc", wc_ref), ("xv", x_ref),
        ("wo", wo_ref), ("wu", wu_ref), ("wd", wd_ref), ("dy", dy_ref),
    ):
        held = getattr(r, "dyv" if name == "dy" else name)
        load[name] = pltpu.make_async_copy(ref, held, r.load.at[len(load)])
        load[name].start()
    xv, dyv = r.xv, r.dyv

    lane = lax.broadcasted_iota(jnp.int32, (1, 128), 1)
    low = (lane < 64).astype(F32)
    high = 1.0 - low
    lowb, highb = low.astype(BF), high.astype(BF)
    hm = (lowb, highb)
    first_core = core == 0

    tmp = r.tmp

    def unpack(name, height, width):
        load[name].wait()
        ref = getattr(r, name)
        lines = height * width // 128
        tmp[0:lines, :] = ref[...].astype(F32)
        step = width // 128
        return [tmp[pl.ds(j, height, stride=step), :].astype(BF) for j in range(step)]

    own = (at["a"], at["o"], at["i"], core)
    agq, ago, agu, agd = r.agq, r.ago, r.agu, r.agd
    for w, ref in enumerate(("wq", "wk", "wv", "wc")):
        blk = unpack(ref, 16, 512)
        for j in range(2):
            cols = slice(w * 256 + j * 128, w * 256 + j * 128 + 128)
            agq[own + (slice(None), cols)] = jnp.where(first_core, blk[j], blk[2 + j])
            r.sendq[:, cols] = jnp.where(first_core, blk[2 + j], blk[j])
    for ref, buf, height, width in (("wo", ago, 16, 512), ("wu", agu, 16, FF), ("wd", agd, 64, 512)):
        for j, blk in enumerate(unpack(ref, height, width)):
            buf[own + (slice(None), slice(j * 128, j * 128 + 128))] = blk

    load["xv"].wait()
    x = xv[...].reshape(256, 512).astype(F32)
    unit, inv = norm_rows(x)
    r.unit1[...] = unit
    r.inv1[...] = jnp.broadcast_to(inv, (256, 128))
    n1own = (unit * ga_ref[...]).astype(BF)
    norm1 = r.norm1
    for b in range(SEQB):
        norm1[b, core] = n1own[b * TOK : (b + 1) * TOK]
    mini = r.mini
    mini[core, 0:2, :] = seg_ref[...].astype(F32)
    mini[core, 2:4, :] = pad_ref[...].astype(F32)
    mini[core, 4:8, :] = jnp.zeros((4, 128), F32)

    pl.semaphore_wait(barrier, len(greet))

    swap_w = remote(r.sendq, agq.at[own], mate)
    swap_m = remote(mini.at[core], mini.at[core], mate)
    swap_n = remote(norm1.at[:, core], norm1.at[:, core], mate)

    def gather(buf, axis, done, lo, width):
        cols = pl.ds(lo, width)
        index = tuple(slice(None) if d in done else pl.ds(at[d], 1) for d in AXES)
        ref = buf.at[index + (slice(None), cols)]
        return [
            remote(ref, ref, device(**{axis: lax.rem(at[axis] + k, size[axis])}))
            for k in range(1, size[axis])
        ]

    swap_w.wait_recv()
    flying, done = {}, ["c" if part[0] == "agq" else "" for part in GATHER]

    def go_on(n):
        buf, lo, width, order = GATHER[n]
        if n in flying:
            arrived(flying.pop(n))
        left = [d for d in order + "c" if d not in done[n]]
        if left:
            flying[n] = gather(getattr(r, buf), left[0], done[n], lo, width)
            done[n] += left[0]

    sums = []

    agenda = iter(SCHEDULE)

    def point():
        for n in next(agenda):
            if n < len(GATHER):
                go_on(n)
            else:
                sums[n - len(GATHER)].advance()

    point()
    arrived([swap_m, swap_n])
    point()
    r.norm1t[...] = norm1[...].reshape(512, 512).T

    turned = [mini[s].T for s in range(2)]
    big_row = lax.broadcasted_iota(jnp.int32, (256, 256), 0)
    big_col = lax.broadcasted_iota(jnp.int32, (256, 256), 1)
    for b in range(SEQB):
        seg_row = jnp.concatenate([mini[0, b : b + 1, :], mini[1, b : b + 1, :]], axis=1)
        seg_col = jnp.concatenate([t[:, b : b + 1] for t in turned], axis=0)
        pad_col = jnp.concatenate([t[:, 2 + b : 3 + b] for t in turned], axis=0)
        same = seg_col == seg_row
        r.mask[b] = jnp.where(same & (big_row >= big_col), 1.0, 0.0)
        r.maskt[b] = jnp.where(same & (big_row <= big_col), 1.0, 0.0)
        seg_last = seg_row[:, 255:256]
        r.last[b] = jnp.broadcast_to((seg_col == seg_last).astype(F32), (256, 128))
        r.padb[b] = jnp.broadcast_to(pad_col, (256, 128))
        r.info[4 + b : 5 + b, :] = jnp.broadcast_to(seg_last, (1, 128))
        r.info[6 + b : 7 + b, :] = jnp.broadcast_to(seg_row[:, 0:1], (1, 128))

    def project(w):
        point()
        mat = agq[..., w * 256 : w * 256 + 256].reshape(512, 256)
        for b in range(SEQB):
            out = nn(norm1[b].reshape(256, 512), mat)
            for pair in range(2):
                part = out[:, pair * 128 : pair * 128 + 128]
                n = b * 2 + pair
                if w == 3:
                    weight = jnp.exp(part) * r.padb[b]
                    r.w[n] = weight
                    r.whi[n], r.wlo[n] = halves(weight)
                else:
                    (r.q, r.k, r.v)[w][n] = part.astype(BF)

    for w in (3, 1, 2):
        project(w)

    def fold(full):
        return full[0:64] * low + full[64:128] * high

    def put_state(ref, n, which, value):
        for t in range(per):
            ref[(n * 2 + which) * per + t, 0:rows, :] = value[t * rows : (t + 1) * rows].astype(ref.dtype)

    def get_block(ref, n, which):
        value = ref[pl.ds((n * 2 + which) * per, per)].astype(F32).reshape(64, 128)
        return jnp.concatenate([value * low, value * high], axis=0)

    def local_state(n, carry):
        weight = r.w[n] * r.last[n // 2]
        hi, lo = halves(weight)
        for which, rhs in enumerate((r.k[n], r.v[n])):
            put_state(r.sloc, n, which, fold(tn(hi, rhs) + tn(lo, rhs)))
        r.info[pl.ds(n, 1), :] = jnp.sum(weight, axis=0, keepdims=True)
        return carry

    point()
    lax.fori_loop(0, 4, local_state, 0)

    def spread(src, dst, info):
        for t in range(nch):
            src[t, rows:, :] = info
        dst[chip] = src[chip]
        return [
            remote(src.at[lax.rem(chip + k, nch)], dst.at[chip], chip_device(lax.rem(chip + k, nch)))
            for k in range(1, nch)
        ]

    def back(src, dst):
        dst[chip] = src[chip]
        return [
            remote(src.at[lax.rem(chip + k, nch)], dst.at[chip], chip_device(lax.rem(chip + k, nch)))
            for k in range(1, nch)
        ]

    point()
    out_1 = spread(r.sloc, r.rcv, r.info[...])

    project(0)

    def mix_local(n, carry):
        q, k, whi, wlo = r.q[n], r.k[n], r.whi[n], r.wlo[n]
        mask = r.mask[n // 2]
        num = jnp.zeros((256, 128), F32)
        for m in hm:
            hi, lo = halves(nt(q * m, k) * mask)
            num += nn(hi, whi * m) + nn(lo, whi * m) + nn(hi, wlo * m)
        r.num[n] = num
        maskb = mask.astype(BF)
        r.tot[n] = nn(maskb, whi) + nn(maskb, wlo)
        return carry

    point()
    lax.fori_loop(0, 4, mix_local, 0)
    point()

    arrived(out_1)
    point()
    rcv = r.rcv
    owned = (chip * rows) // 256

    def last_of(p, b):
        return rcv[p, pl.ds(rows + 4 + b, 1), :]

    def first_of(p, b):
        return rcv[p, pl.ds(rows + 6 + b, 1), :]

    run = jnp.zeros((rows, 128), F32)
    for p in range(nch):
        r.snd[p] = run
        if p == 0:
            run = rcv[0, 0:rows, :]
        else:
            keep = (last_of(p - 1, owned) == last_of(p, owned)).astype(F32)
            run = rcv[p, 0:rows, :] + keep * run
    point()
    out_2 = back(r.snd, r.stin)
    point()
    zrun = [jnp.zeros((2, 128), F32) for _ in range(SEQB)]
    for p in range(nch - 1):
        for b in range(SEQB):
            z = rcv[p, rows + 2 * b : rows + 2 * b + 2, :]
            if p > 0:
                z = z + (last_of(p - 1, b) == last_of(p, b)).astype(F32) * zrun[b]
            zrun[b] = jnp.where(p < chip, z, zrun[b])
    before = jnp.maximum(chip - 1, 0)
    for b in range(SEQB):
        r.zin[2 * b : 2 * b + 2, :] = zrun[b]
        open_doc = jnp.where(chip > 0, last_of(before, b), -1.0)[:, 0:1]
        seg_col = jnp.concatenate([t[:, b : b + 1] for t in turned], axis=0)
        r.use[b] = jnp.broadcast_to((seg_col == open_doc).astype(F32), (256, 128))

    point()
    arrived(out_2)

    def both(op, v):
        if op is jnp.max:
            a = jnp.max(jnp.where(lane < 64, v, -jnp.inf), axis=1, keepdims=True)
            b = jnp.max(jnp.where(lane < 64, -jnp.inf, v), axis=1, keepdims=True)
        else:
            a = jnp.sum(v * low, axis=1, keepdims=True)
            b = jnp.sum(v * high, axis=1, keepdims=True)
        return jnp.where(lane < 64, a, b)

    def mix_rest(n, carry):
        b = n // 2
        q, v, whi = r.q[n], r.v[n], r.whi[n]
        mask, use = r.mask[b], r.use[b]
        khi, klo = halves(get_block(r.stin, n, 0))
        num = r.num[n] + use * (nt(q, khi) + nt(q, klo))
        tot = r.tot[n] + use * r.zin[pl.ds(n, 1), :]
        floor = jnp.maximum(tot, 1.0)
        score = num / (floor * 8.0)
        e = jnp.exp(score - both(jnp.max, score))
        share = e / (both(jnp.sum, e) * floor)
        r.tot[n] = tot
        r.score[n] = score
        r.share[n] = share
        sb = share.astype(BF)
        out = use * nn(sb, get_block(r.stin, n, 1).astype(BF))
        for m in hm:
            out += nn((nt(sb * m, whi) * mask).astype(BF), v * m)
        r.outb[n] = out.astype(BF).reshape(2, TOK, 128)
        return carry

    point()
    lax.fori_loop(0, 4, mix_rest, 0)
    point()
    swap_o = remote(r.outb.at[:, 1 - core], r.mixx.at[core], mate)
    for n in range(4):
        r.mixx[core, n] = r.outb[n, core]

    point()
    swap_o.wait_recv()
    point()
    mixx = r.mixx
    for b in range(SEQB):
        r.mixed[b * TOK : (b + 1) * TOK, :] = jnp.concatenate(
            [mixx[h, b * 2 + p] for h in range(2) for p in range(2)], axis=1
        )
    w_out = ago[...].reshape(512, 512)
    residual = xv[...].reshape(256, 512).astype(F32) + nn(r.mixed[...], w_out)
    r.res[...] = residual
    unit, inv = norm_rows(residual)
    r.unit2[...] = unit
    r.inv2[...] = jnp.broadcast_to(inv, (256, 128))
    r.n2[...] = (unit * gf_ref[...]).astype(BF)
    r.n2t[...] = r.n2[...].T

    class Sum:
        def __init__(self, name, buffer, order, width, height, lo, emit):
            self.emit = emit
            self.name, self.order, self.width, self.height = name, order, width, height
            self.ref, self.lo, self.dims, self.step = getattr(r, buffer), lo, list(AXES), 0
            self.going = False

        def start(self):
            ax = self.order[self.step]
            p = self.dims.index(ax)
            cols = pl.ds(self.lo, self.width)
            land = getattr(r, f"r{self.name}_{self.step}")
            self.copies, self.going = [], True
            for k in range(1, size[ax]):
                to = lax.rem(at[ax] + k, size[ax])
                index = [slice(None)] * len(self.dims) + [slice(None), cols]
                index[p] = to
                self.copies.append(remote(self.ref.at[tuple(index)], land.at[k - 1], device(**{ax: to})))

        def advance(self):
            if self.going:
                self.finish()
            if self.step < len(self.order):
                self.start()

        def finish(self):
            emit = self.emit if self.step == len(self.order) - 1 else None
            ax = self.order[self.step]
            p = self.dims.index(ax)
            arrived(self.copies)
            land = getattr(r, f"r{self.name}_{self.step}")
            cols = slice(self.lo, self.lo + self.width)
            left = [size[d] for d in self.dims if d != ax]
            total = 1
            for extent in left:
                total *= extent
            into = None if emit else getattr(r, f"s{self.name}_{self.step}")

            def one(flat):
                index, rest_of = [], flat
                for extent in reversed(left):
                    index.insert(0, rest_of % extent if isinstance(rest_of, int) else lax.rem(rest_of, extent))
                    rest_of = rest_of // extent
                full = list(index)
                full.insert(p, at[ax])
                value = self.ref[tuple(full) + (slice(None), cols)].astype(F32)
                for k in range(size[ax] - 1):
                    value += land[(k,) + tuple(index)].astype(F32)
                if emit:
                    emit(index, value)
                else:
                    into[tuple(index)] = value.astype(BF)

            if total <= 2:
                for flat in range(total):
                    one(flat)
            else:
                def body(flat, carry):
                    one(flat)
                    return carry

                lax.fori_loop(0, total, body, 0)
            self.dims.remove(ax)
            self.ref, self.lo, self.step = into, 0, self.step + 1

    def to_rows(out_ref, height, width, lo):
        def emit(index, value):
            step = width // 128
            for j in range(value.shape[1] // 128):
                out_ref[pl.ds(lo // 128 + j, height, stride=step), :] = value[:, j * 128 : j * 128 + 128]

        return emit

    shards = {}

    def to_core(name):
        def emit(index, value):
            shards[name, index[0]] = value
            if index[0] == 1:
                at_lo = slice(PIECE[name][2], PIECE[name][2] + 256)
                halves_of = (shards[name, 0], shards[name, 1])
                r.final[core, :, at_lo] = jnp.where(first_core, *halves_of)
                r.fsend[:, at_lo] = jnp.where(first_core, *reversed(halves_of))

        return emit

    outs = dict(go=(oo_ref, 16, 512), gu=(ou_ref, 16, FF), gd=(od_ref, 64, 512))
    for name, (buf, order, lo, width, height) in enumerate(PIECE):
        emit = to_core(name) if buf == "gq" else to_rows(*outs[buf], lo)
        sums.append(Sum(name, buf, order, width, height, lo, emit))

    load["dy"].wait()
    dy = dyv[...].reshape(256, 512)
    span = na * OUTER // 4
    for j in range(4):
        point()
        cols = slice(j * 512, j * 512 + 512)
        pre = nn(r.n2[...], agu[:, :, :, :, :, cols].reshape(512, 512))
        sig = 1.0 / (1.0 + jnp.exp(-pre))
        hidden = (pre * sig).astype(BF)
        r.hidden[:, cols] = hidden
        r.dsilu[:, cols] = sig * (1.0 + pre * (1.0 - sig))
        block = (j * span // OUTER, slice(j * span % OUTER, j * span % OUTER + span))
        r.gd[block] = tn(hidden, dy).astype(BF).reshape((span, ni, 2, 64, 512))
    for j in range(4):
        point()
        cols = slice(j * 512, j * 512 + 512)
        block = (j * span // OUTER, slice(j * span % OUTER, j * span % OUTER + span))
        d_pre = (nt(dy, agd[block].reshape(512, 512)) * r.dsilu[:, cols]).astype(BF)
        part = nt(d_pre, agu[:, :, :, :, :, cols].reshape(512, 512))
        r.dn2[...] = part if j == 0 else r.dn2[...] + part
        r.gu[:, :, :, :, :, cols] = nn(r.n2t[...], d_pre).astype(BF).reshape((na, OUTER, ni, 2, 16, 512))
    point()

    dn2 = r.dn2[...]
    unit = r.unit2[...]
    gains2 = jnp.sum(dn2 * unit, axis=0, keepdims=True)
    d_res = dy.astype(F32) + norm_back(
        dn2 * gf_ref[...], unit, r.inv2[:, 0:1]
    )
    r.dres[...] = d_res
    d_attn = d_res.astype(BF)
    d_mixed = nt(d_attn, w_out).astype(BF)
    for b in range(SEQB):
        for p in range(2):
            part = [d_mixed[b * TOK : (b + 1) * TOK, h * 256 + p * 128 : h * 256 + p * 128 + 128] for h in range(2)]
            r.do[b * 2 + p, core] = jnp.where(first_core, part[0], part[1])
            r.senddo[b * 2 + p] = jnp.where(first_core, part[1], part[0])
    point()
    swap_d = remote(r.senddo, r.do.at[:, core], mate)
    point()
    swap_d.wait_recv()

    def mix_back(n, carry):
        b = n // 2
        q, v, whi = r.q[n], r.v[n], r.whi[n]
        mask, use = r.mask[b], r.use[b]
        share, tot, score = r.share[n], r.tot[n], r.score[n]
        d_out = r.do[n].reshape(256, 128)
        ds = use * nt(d_out, get_block(r.stin, n, 1).astype(BF))
        for m in hm:
            ds += nn((nt(d_out * m, v) * mask).astype(BF), whi * m)
        floor = jnp.maximum(tot, 1.0)
        inv_floor = 1.0 / floor
        prob = share * floor
        dprob = ds * inv_floor
        dscore = prob * (dprob - both(jnp.sum, dprob * prob))
        dnum = dscore * inv_floor * 0.125
        gate = jnp.where(tot > 1.0, 1.0, jnp.where(tot == 1.0, 0.5, 0.0))
        dtot = -(ds * share + dscore * score) * inv_floor * gate
        r.dnum[n] = dnum.astype(BF)
        r.dtot[n] = dtot
        put_state(r.dloc, n, 0, fold(tn((use * dnum).astype(BF), q)))
        put_state(r.dloc, n, 1, fold(tn((use * share).astype(BF), d_out)))
        r.gz[pl.ds(n, 1), :] = jnp.sum(use * dtot, axis=0, keepdims=True)
        return carry

    point()
    lax.fori_loop(0, 4, mix_back, 0)
    point()
    r.gz[4:8, :] = jnp.zeros((4, 128), F32)
    gz_parts = jnp.concatenate(halves(r.gz[...]), axis=0)
    out_3 = spread(r.dloc, r.drcv, gz_parts)

    point()
    r.go[...] = tn(r.mixed[...], d_attn).astype(BF).reshape((na, OUTER, ni, 2, 16, 512))
    point()
    y_rows = r.res[...] + nn(r.hidden[...], agd[...].reshape(FF, 512))
    y_ref[...] = y_rows.astype(BF).reshape(SEQB, TOK, 512)

    def mix_back_local(n, carry):
        b = n // 2
        q, k, v, whi, w = r.q[n], r.k[n], r.v[n], r.whi[n], r.w[n]
        mask, maskt, use = r.mask[b], r.maskt[b], r.use[b]
        d_out, dnum = r.do[n].reshape(256, 128), r.dnum[n]
        sb = r.share[n].astype(BF)
        dq = use * nn(dnum, get_block(r.stin, n, 0).astype(BF))
        dk = jnp.zeros((256, 128), F32)
        dv = jnp.zeros((256, 128), F32)
        dw = nn(maskt.astype(BF), r.dtot[n].astype(BF))
        for m in hm:
            dq += nn((nt(dnum * m, whi) * mask).astype(BF), k * m)
            dk += nn((nt(whi * m, dnum) * maskt).astype(BF), q * m)
            dv += nn((nt(whi * m, sb) * maskt).astype(BF), d_out * m)
            dw += nn((nt(v * m, d_out) * maskt).astype(BF), sb * m)
            dw += nn((nt(k * m, q) * maskt).astype(BF), dnum * m)
        cols = pl.ds(pl.multiple_of(lax.rem(n, 2) * 128, 128), 128)
        r.dd[b, :, :, cols] = dq.astype(BF).reshape(2, TOK, 128)
        r.dkl[n] = dk
        r.dvl[n] = dv
        r.dwl[n] = dw
        return carry

    point()
    lax.fori_loop(0, 4, mix_back_local, 0)
    dd = r.dd

    def weight_gradient(lo, width):
        value = nn(r.norm1t[...], dd[:, :, :, lo : lo + width].reshape(512, width))
        r.gq[:, :, :, :, :, lo : lo + width] = value.astype(BF).reshape((na, OUTER, ni, 2, 16, width))

    point()
    weight_gradient(0, 256)
    point()

    arrived(out_3)
    point()
    drcv = r.drcv
    run = jnp.zeros((rows, 128), F32)
    for p in reversed(range(nch)):
        r.dsnd[p] = run.astype(BF)
        here = drcv[p, 0:rows, :].astype(F32)
        if p == nch - 1:
            run = here
        else:
            run = here + (first_of(p, owned) == first_of(p + 1, owned)).astype(F32) * run
    point()
    out_4 = back(r.dsnd, r.gin)
    point()
    zrun = [jnp.zeros((2, 128), F32) for _ in range(SEQB)]
    for p in reversed(range(1, nch)):
        for b in range(SEQB):
            tail = drcv[p, rows : rows + 16, :].astype(F32)
            z = tail[2 * b : 2 * b + 2] + tail[8 + 2 * b : 10 + 2 * b]
            if p < nch - 1:
                z = z + (first_of(p, b) == first_of(p + 1, b)).astype(F32) * zrun[b]
            zrun[b] = jnp.where(p > chip, z, zrun[b])
    after = jnp.minimum(chip + 1, nch - 1)
    for b in range(SEQB):
        r.gz[2 * b : 2 * b + 2, :] = zrun[b]
        matched = (first_of(after, b) == r.info[4 + b : 5 + b, :]) & (chip < nch - 1)
        r.last[b] = r.last[b] * matched.astype(F32)
    point()
    arrived(out_4)
    point()

    def mix_last(n, carry):
        b = n // 2
        k, v, whi, w, last = r.k[n], r.v[n], r.whi[n], r.w[n], r.last[b]
        gk = get_block(r.gin, n, 0).astype(BF)
        gv = get_block(r.gin, n, 1).astype(BF)
        dk = r.dkl[n] + last * nn(whi, gk)
        dv = r.dvl[n] + last * nn(whi, gv)
        dw = r.dwl[n] + last * (nt(k, gk) + nt(v, gv) + r.gz[pl.ds(n, 1), :])
        for slot, value in ((1, dk), (2, dv), (3, dw * w)):
            cols = pl.ds(pl.multiple_of(slot * 256 + lax.rem(n, 2) * 128, 128), 128)
            dd[b, :, :, cols] = value.astype(BF).reshape(2, TOK, 128)
        return carry

    lax.fori_loop(0, 4, mix_last, 0)
    for name, lo in (("kg", 256), ("vg", 512), ("cg", 768)):
        point()
        weight_gradient(lo, 256)

    point()
    full_q = agq[...].reshape(512, 1024)
    for b in range(SEQB):
        part = nt(dd[b].reshape(256, 1024), full_q)
        r.dn1[:, b] = part.reshape(2, TOK, 512)
    point()
    swap_g = remote(r.dn1.at[1 - core], r.dn1r, mate)

    point()
    swap_g.wait_recv()
    point()
    dn1 = (r.dn1[core] + r.dn1r[...]).reshape(256, 512)
    unit = r.unit1[...]
    gains1 = jnp.sum(dn1 * unit, axis=0, keepdims=True)
    dx = r.dres[...] + norm_back(dn1 * ga_ref[...], unit, r.inv1[:, 0:1])
    dx_ref[...] = dx.astype(BF).reshape(SEQB, TOK, 512)

    gains = jnp.concatenate(
        [g[:, j * 128 : j * 128 + 128] for g in (gains1, gains2) for j in range(4)], axis=0
    )

    def exchange(buf, value, me, count, dev):
        buf[me] = value
        return [remote(buf.at[me], buf.at[me], dev(lax.rem(me + k, count))) for k in range(1, count)]

    def total(buf, copies, count):
        arrived(copies)
        value = buf[0]
        for k in range(1, count):
            value = value + buf[k]
        return value

    point()
    copies = exchange(r.gain1, gains, core, 2, lambda t: device(c=t))
    point()
    gains = total(r.gain1, copies, 2)
    point()
    copies = exchange(r.gain2, gains, chip, nch, chip_device)
    point()
    gains = total(r.gain2, copies, nch)
    point()
    copies = exchange(r.gain3, gains, at["a"], na, lambda t: device(a=t))

    final = r.final
    point()
    swap_f = remote(r.fsend, final.at[core], mate)
    point()
    gains = total(r.gain3, copies, na)
    for ref, first in ((og1_ref, 0), (og2_ref, 4)):
        for j in range(4):
            ref[:, j * 128 : j * 128 + 128] = gains[first + j : first + j + 1]
    point()
    swap_f.wait_recv()
    for ref, lo in ((oq_ref, 0), (ok_ref, 256), (ov_ref, 512), (oc_ref, 768)):
        for j in range(4):
            ref[pl.ds(j, 16, stride=4), :] = final[j // 2, :, lo + (j % 2) * 128 : lo + (j % 2) * 128 + 128]
    point()
    for copy in started:
        copy.wait_send()


def hand_over(count, *refs):
    src, dst, held, sems = refs[:count], refs[count : 2 * count], refs[2 * count : 3 * count], refs[3 * count]
    into = [pltpu.make_async_copy(src[n], held[n], sems.at[0, n]) for n in range(count)]
    away = [pltpu.make_async_copy(held[n], dst[n], sems.at[1, n]) for n in range(count)]
    for copy in into:
        copy.start()
    for n in range(count):
        into[n].wait()
        away[n].start()
    for copy in away:
        copy.wait()


def solution(mesh):
    ndp, nseq = mesh.shape["dp"], mesh.shape["seq"]
    joint = D // (ndp * nseq) >= 16
    na = ndp if joint else 1
    ni = nseq // (2 * OUTER)
    scratch = layout(na, ni)
    names = tuple(scratch)
    both_axes = ("dp", "seq")

    def body(x, dy, seg, pad, *args):
        weights, (gain_attn, gain_ffn) = args[:7], args[7:]
        shards = []
        for w in weights:
            if not joint:
                whole = lax.all_gather(w, both_axes, axis=0, tiled=True).reshape(nseq, -1)
                w = lax.dynamic_index_in_dim(whole, lax.axis_index("seq"), 0, keepdims=False)
            shards.append(w.reshape(-1, 128))
        outs = [jax.ShapeDtypeStruct(x.shape, BF)] * 2
        outs += [jax.ShapeDtypeStruct(w.shape, F32) for w in shards]
        outs += [jax.ShapeDtypeStruct((1, D), F32)] * 2
        vmem, hbm = pl.BlockSpec(memory_space=pltpu.VMEM), pl.BlockSpec(memory_space=pltpu.HBM)
        got = pl.pallas_call(
            functools.partial(kernel, na, ni, names),
            out_shape=outs,
            in_specs=[hbm] * 2 + [vmem] * 2 + [hbm] * 7 + [vmem] * 2,
            out_specs=[vmem] * 11,
            scratch_shapes=list(scratch.values()),
            compiler_params=pltpu.CompilerParams(
                collective_id=0, has_side_effects=True, vmem_limit_bytes=62 * 2**20
            ),
            cost_estimate=pl.CostEstimate(flops=12 * 10**9, bytes_accessed=4 * 2**20, transcendentals=10**6),
            name="block",
        )(x, dy, seg, pad, *shards, gain_attn.reshape(1, D), gain_ffn.reshape(1, D))
        got = pl.pallas_call(
            functools.partial(hand_over, 11),
            out_shape=outs,
            in_specs=[hbm] * 11,
            out_specs=[hbm] * 11,
            scratch_shapes=[pltpu.VMEM(o.shape, o.dtype) for o in outs] + [pltpu.SemaphoreType.DMA((2, 11))],
            name="results",
        )(*got)
        y, dx = got[:2]
        grads = [g.reshape(-1) for g in got[2:9]]
        gains = [g.reshape(-1) for g in got[9:]]
        if not joint:
            index = lax.axis_index("dp") * nseq + lax.axis_index("seq")
            grads = [lax.psum(g, "dp") for g in grads]
            grads = [lax.all_gather(g, "seq", axis=0, tiled=True) for g in grads]
            grads = [
                lax.dynamic_slice_in_dim(g, index * (g.shape[0] // (ndp * nseq)), g.shape[0] // (ndp * nseq))
                for g in grads
            ]
            gains = [lax.psum(g, "dp") for g in gains]
        return (y, dx, *grads, *gains)

    data, ids, flat = P("dp", "seq", None), P("dp", "seq"), P(("dp", "seq"))
    return jax.shard_map(
        body,
        mesh=mesh,
        in_specs=(data, data, ids, ids) + (flat,) * 7 + (P(), P()),
        out_specs=(data, data) + (flat,) * 7 + (P(), P()),
        check_vma=False,
    )
```

time: 133 us -> 104 us (0.78)
  Pallas kernels: 123 us -> 103 us
  local copies, waits for them, and re-layouts: 8.6 us -> 0 us
    pallas_call x1, Pallas kernels: 123 us -> 101 us  [body(): pl.pallas_call(functools.partial(kernel, na, ni, names), out_shape=outs,...]
    unnamed x31 -> x0, local copies, waits for them, and re-layouts: 8.6 us -> none
    pallas_call x0 -> x1, Pallas kernels: none -> 2.08 us  [body(): pl.pallas_call(functools.partial(hand_over, 11), out_shape=outs, in_specs...]
where the time goes in v2:
time: 104 us
  Pallas kernels  103 us (99%)
    pallas_call x1, Pallas kernels, body(): pl.pallas_call(functools.partial(kernel, na, ni, names), out_shape=outs,...  101 us
    pallas_call x1, Pallas kernels, body(): pl.pallas_call(functools.partial(hand_over, 11), out_shape=outs, in_specs...  2.08 us

profile of v2, /device:TPU:0, one launch (start us, length us, event | category | flops | bytes accessed | tf_op | source)
XLA Modules:
  0.0 103.8 jit_solution(17514707116343143695)
XLA Ops:
  0.6 101.1 %block.1 = (bf16[2,128,512]{2,1,0:T(8,128)(2,1)}, bf16[2,128,512]{2,1,0:T(8,128)(2,1)}, f32[64,128]{1,0:T(8,128)}, f32[64,128]{1,0:T(8,128)}, f32[64,128]{1,0:T(...) custom-call(bf16[2,128,512]{2,1,0:T(8,128)(2,1)} %refs_0_.1, ...), custom_call_target="tpu_custom_call" | custom-call | flops 12000000000 | bytes 4194304 | tf_op jit(solution)/shard_map/block/pallas_call | solution.py:903
  101.8 2.1 %results.1 = (bf16[2,128,512]{2,1,0:T(8,128)(2,1)}, bf16[2,128,512]{2,1,0:T(8,128)(2,1)}, f32[64,128]{1,0:T(8,128)}, f32[64,128]{1,0:T(8,128)}, f32[64,128]{1,0:...) custom-call(bf16[2,128,512]{2,1,0:T(8,128)(2,1)} %get-tuple-element., ...), custom_call_target="tpu_custom_call" | custom-call | tf_op jit(solution)/shard_map/results/pallas_call | solution.py:915

commit v3 on v2

--- a/solution.py
+++ b/solution.py
@@ -17,97 +17,99 @@
 F32 = jnp.float32
 EPS = 1e-05
 MESH = pl.DeviceIdType.MESH
-AXES = "aoic"
+AXES = "apric"
 
 
 GATHER = (
-    ("agq", 768, 256, "oia"),
-    ("agq", 256, 256, "oai"),
-    ("agq", 512, 256, "oia"),
-    ("agq", 0, 256, "oia"),
-    ("ago", 0, 512, "oai"),
-    ("agu", 0, 512, "ioa"),
-    ("agu", 512, 512, "ioa"),
-    ("agu", 1024, 512, "oai"),
-    ("agu", 1536, 512, "aoi"),
-    ("agd", 0, 128, "oia"),
-    ("agd", 128, 128, "oai"),
-    ("agd", 256, 128, "aio"),
-    ("agd", 384, 128, "oia"),
+    ("agq", 768, 256, "rpia"),
+    ("agq", 256, 256, "pari"),
+    ("agq", 512, 256, "rpia"),
+    ("agq", 0, 256, "apri"),
+    ("ago", 0, 512, "piar"),
+    ("agu", 0, 512, "pira"),
+    ("agu", 512, 512, "rpai"),
+    ("agu", 1024, 512, "iapr"),
+    ("agu", 1536, 512, "ipar"),
+    ("agd", 0, 128, "pria"),
+    ("agd", 128, 128, "rpai"),
+    ("agd", 256, 128, "prai"),
+    ("agd", 384, 128, "prai"),
 )
 PIECE = (
-    ("gq", "aio", 0, 256, 16),
-    ("gq", "iao", 256, 256, 16),
-    ("gq", "aio", 512, 256, 16),
-    ("gq", "aio", 768, 256, 16),
-    ("go", "ciao", 0, 512, 16),
-    ("gu", "ciao", 0, 512, 16),
-    ("gu", "cioa", 512, 512, 16),
-    ("gu", "caoi", 1024, 512, 16),
-    ("gu", "caio", 1536, 512, 16),
-    ("gd", "cioa", 0, 128, 64),
-    ("gd", "caoi", 128, 128, 64),
-    ("gd", "coia", 256, 128, 64),
-    ("gd", "cioa", 384, 128, 64),
+    ("gq", "iarp", 0, 256, 16),
+    ("gq", "airp", 256, 256, 16),
+    ("gq", "iarp", 512, 256, 16),
+    ("gq", "raip", 768, 256, 16),
+    ("go", "cripa", 0, 512, 16),
+    ("gu", "cripa", 0, 512, 16),
+    ("gu", "ciarp", 512, 512, 16),
+    ("gu", "capri", 1024, 512, 16),
+    ("gu", "ciapr", 1536, 512, 16),
+    ("gd", "cairp", 0, 128, 64),
+    ("gd", "crapi", 128, 128, 64),
+    ("gd", "cripa", 256, 128, 64),
+    ("gd", "caipr", 384, 128, 64),
 )
 SCHEDULE = (
-    (10, 11, 4, 8, 0, 1, 2, 5, 6, 10, 3, 0, 1, 4, 7, 2, 5, 0),
-    (3, 12, 1, 2, 4, 6, 10, 9, 3, 8, 0),
-    (1,),
-    (),
-    (2,),
-    (),
-    (),
-    (5, 6, 12, 11, 3, 7),
-    (10, 9),
-    (),
-    (),
-    (),
-    (5, 8, 12, 4),
-    (6, 7, 6, 9, 4, 5, 11),
-    (),
-    (),
-    (7, 8),
+    (0, 11, 9),
+    (7, 2, 1),
+    (4, 0, 11, 3, 12, 9, 6, 1, 2, 7, 3, 0, 11, 10, 9, 1, 2, 10, 0, 8, 4, 5, 3, 1, 7, 6, 2, 12, 10, 3, 8, 5, 7, 0, 4),
+    (11, 1),
+    (6, 2),
+    (),
+    (),
+    (9, 7, 12, 3, 4, 5, 10, 8),
+    (),
+    (11,),
+    (),
+    (),
+    (9, 5, 6, 4, 7, 9),
+    (10, 4, 8, 10, 12),
+    (),
+    (),
+    (6, 11, 5, 8, 12),
+    (),
+    (6, 5),
     (),
     (12,),
-    (10, 9, 11),
-    (7,),
-    (11, 8, 12, 9),
-    (),
+    (8,),
     (24,),
-    (22, 19, 23),
-    (),
-    (),
-    (),
-    (19, 24, 22, 23, 25),
-    (),
+    (25,),
+    (),
+    (20,),
     (21,),
     (),
-    (20,),
-    (25, 17, 19, 21, 18),
-    (),
-    (),
-    (),
-    (),
-    (17, 20, 23),
-    (13, 19, 21, 22),
-    (),
-    (),
-    (14, 17),
-    (20,),
-    (16,),
-    (13,),
-    (25, 24, 15),
-    (18,),
-    (21, 14, 16),
-    (17,),
-    (24, 22, 23, 13, 15, 25),
-    (18, 14, 16, 15, 21),
-    (19, 25, 18, 14, 23, 20, 16, 24),
-    (17, 15, 13, 22),
-    (),
-    (),
-    (20, 18),
+    (25, 23, 20, 24, 21),
+    (),
+    (),
+    (18, 23),
+    (),
+    (),
+    (),
+    (),
+    (24,),
+    (18, 23, 19),
+    (),
+    (13, 22, 21, 20),
+    (25, 17),
+    (22, 24),
+    (15,),
+    (21, 17),
+    (),
+    (19, 14),
+    (20, 16, 18),
+    (13, 15),
+    (25, 17, 14),
+    (21, 19, 23),
+    (),
+    (),
+    (),
+    (24, 15, 16, 22, 13, 18, 17, 20, 14),
+    (19, 15, 16, 13, 22, 14, 25, 18),
+    (19, 16, 24, 22, 15, 17, 23, 21, 14, 13, 20, 16),
+    (19, 17, 23, 25, 18),
+    (),
+    (22,),
 )
 
 
@@ -143,7 +145,7 @@
 def layout(na, ni):
     nch = OUTER * ni
     rows = 512 // nch
-    lead = (na, OUTER, ni, 2)
+    lead = (na, 2, 2, ni, 2)
     s = {}
 
     def vm(name, shape, dtype):
@@ -155,8 +157,8 @@
     vm("ago", lead + (16, 512), BF)
     vm("agu", lead + (16, FF), BF)
     vm("agd", lead + (64, 512), BF)
-    vm("unit1", (256, 512), F32)
-    vm("inv1", (256, 128), F32)
+    vm("unit1", (SEQB, 2, TOK, 512), F32)
+    vm("inv1", (SEQB, 2, TOK, 128), F32)
     vm("norm1", (SEQB, 2, TOK, 512), BF)
     vm("mini", (2, 8, 128), F32)
     for m in ("mask", "maskt"):
@@ -169,10 +171,14 @@
         vm(m, (4, 256, 128), F32)
     vm("dnum", (4, 256, 128), BF)
     vm("info", (8, 128), F32)
-    for m, kind, extra in (("sloc", F32, 8), ("rcv", F32, 8), ("dloc", BF, 16), ("drcv", BF, 16)):
+    for m, kind, extra in (("dloc", BF, 16), ("drcv", BF, 16)):
         vm(m, (nch, rows + extra, 128), kind)
-    for m, kind in (("snd", F32), ("stin", F32), ("dsnd", BF), ("gin", BF)):
-        vm(m, (nch, rows, 128), kind)
+    for m in ("dsnd", "gin"):
+        vm(m, (nch, rows, 128), BF)
+    third = 256 // nch
+    for m, extra in (("sloc", 16), ("rcv", 16), ("snd", 0), ("stin", 0)):
+        vm(m, (nch, 3 * third + extra, 128), BF)
+    vm("infos", (nch, 8, 128), F32)
     vm("zin", (8, 128), F32)
     vm("gz", (8, 128), F32)
     vm("outb", (4, 2, TOK, 128), BF)
@@ -186,7 +192,7 @@
     vm("norm1t", (512, 512), BF)
     vm("hidden", (256, FF), BF)
     vm("dsilu", (256, FF), F32)
-    vm("xv", (SEQB, TOK, 512), BF)
+    vm("xall", (SEQB, 2, TOK, 512), BF)
     vm("dyv", (SEQB, TOK, 512), BF)
     for name, lines in (("wq", 64), ("wk", 64), ("wv", 64), ("wc", 64), ("wo", 64), ("wu", 256), ("wd", 256)):
         vm(name, (lines, 128), BF)
@@ -206,7 +212,7 @@
     for name, (_, order, _, width, height) in enumerate(PIECE):
         dims = list(AXES)
         for step, ax in enumerate(order):
-            size = dict(a=na, o=OUTER, i=ni, c=2)
+            size = dict(a=na, p=2, r=2, i=ni, c=2)
             dims.remove(ax)
             left = tuple(size[d] for d in dims)
             vm(f"r{name}_{step}", (max(size[ax] - 1, 1),) + left + (height, width), BF)
@@ -225,17 +231,26 @@
     nch = OUTER * ni
     rows = 512 // nch
     per = 64 // rows
+    third = 256 // nch
+    share_of = 64 // third
 
     dp = lax.axis_index("dp")
     seq = lax.axis_index("seq")
     chip = seq // 2
-    at = dict(a=dp if na > 1 else 0, o=chip // ni, i=lax.rem(chip, ni), c=lax.rem(seq, 2))
-    size = dict(a=na, o=OUTER, i=ni, c=2)
+    at = dict(
+        a=dp if na > 1 else 0,
+        p=chip // (2 * ni),
+        r=lax.rem(chip // ni, 2),
+        i=lax.rem(chip, ni),
+        c=lax.rem(seq, 2),
+    )
+    size = dict(a=na, p=2, r=2, i=ni, c=2)
+    lead = (na, 2, 2, ni, 2)
     core = at["c"]
 
     def device(**moved):
         p = {**at, **moved}
-        return (p["a"] if na > 1 else dp, (p["o"] * ni + p["i"]) * 2 + p["c"])
+        return (p["a"] if na > 1 else dp, ((p["p"] * 2 + p["r"]) * ni + p["i"]) * 2 + p["c"])
 
     def chip_device(t):
         return (dp, t * 2 + core)
@@ -271,13 +286,13 @@
 
     load = {}
     for name, ref in (
-        ("wq", wq_ref), ("wk", wk_ref), ("wv", wv_ref), ("wc", wc_ref), ("xv", x_ref),
+        ("wq", wq_ref), ("wk", wk_ref), ("wv", wv_ref), ("wc", wc_ref), ("x", x_ref),
         ("wo", wo_ref), ("wu", wu_ref), ("wd", wd_ref), ("dy", dy_ref),
     ):
-        held = getattr(r, "dyv" if name == "dy" else name)
+        held = r.xall.at[:, core] if name == "x" else r.dyv if name == "dy" else getattr(r, name)
         load[name] = pltpu.make_async_copy(ref, held, r.load.at[len(load)])
         load[name].start()
-    xv, dyv = r.xv, r.dyv
+    xall, dyv = r.xall, r.dyv
 
     lane = lax.broadcasted_iota(jnp.int32, (1, 128), 1)
     low = (lane < 64).astype(F32)
@@ -296,7 +311,7 @@
         step = width // 128
         return [tmp[pl.ds(j, height, stride=step), :].astype(BF) for j in range(step)]
 
-    own = (at["a"], at["o"], at["i"], core)
+    own = (at["a"], at["p"], at["r"], at["i"], core)
     agq, ago, agu, agd = r.agq, r.ago, r.agu, r.agd
     for w, ref in enumerate(("wq", "wk", "wv", "wc")):
         blk = unpack(ref, 16, 512)
@@ -308,25 +323,18 @@
         for j, blk in enumerate(unpack(ref, height, width)):
             buf[own + (slice(None), slice(j * 128, j * 128 + 128))] = blk
 
-    load["xv"].wait()
-    x = xv[...].reshape(256, 512).astype(F32)
-    unit, inv = norm_rows(x)
-    r.unit1[...] = unit
-    r.inv1[...] = jnp.broadcast_to(inv, (256, 128))
-    n1own = (unit * ga_ref[...]).astype(BF)
     norm1 = r.norm1
-    for b in range(SEQB):
-        norm1[b, core] = n1own[b * TOK : (b + 1) * TOK]
     mini = r.mini
     mini[core, 0:2, :] = seg_ref[...].astype(F32)
     mini[core, 2:4, :] = pad_ref[...].astype(F32)
     mini[core, 4:8, :] = jnp.zeros((4, 128), F32)
 
+    load["x"].wait()
     pl.semaphore_wait(barrier, len(greet))
 
     swap_w = remote(r.sendq, agq.at[own], mate)
     swap_m = remote(mini.at[core], mini.at[core], mate)
-    swap_n = remote(norm1.at[:, core], norm1.at[:, core], mate)
+    swap_n = remote(xall.at[:, core], xall.at[:, core], mate)
 
     def gather(buf, axis, done, lo, width):
         cols = pl.ds(lo, width)
@@ -363,7 +371,12 @@
     point()
     arrived([swap_m, swap_n])
     point()
-    r.norm1t[...] = norm1[...].reshape(512, 512).T
+    unit, inv = norm_rows(xall[...].reshape(512, 512).astype(F32))
+    r.unit1[...] = unit.reshape(SEQB, 2, TOK, 512)
+    r.inv1[...] = jnp.broadcast_to(inv, (512, 128)).reshape(SEQB, 2, TOK, 128)
+    normed = (unit * ga_ref[...]).astype(BF)
+    norm1[...] = normed.reshape(SEQB, 2, TOK, 512)
+    r.norm1t[...] = normed.T
 
     turned = [mini[s].T for s in range(2)]
     big_row = lax.broadcasted_iota(jnp.int32, (256, 256), 0)
@@ -410,11 +423,20 @@
         value = ref[pl.ds((n * 2 + which) * per, per)].astype(F32).reshape(64, 128)
         return jnp.concatenate([value * low, value * high], axis=0)
 
+    def pack_state(key_sum, value_sum):
+        return jnp.concatenate([*halves(key_sum), value_sum.astype(BF)], axis=0)
+
+    def carried(n, which):
+        value = r.stin[pl.ds(n * share_of, share_of), which * third : (which + 1) * third, :].reshape(64, 128)
+        return jnp.concatenate([value * lowb, value * highb], axis=0)
+
     def local_state(n, carry):
         weight = r.w[n] * r.last[n // 2]
         hi, lo = halves(weight)
-        for which, rhs in enumerate((r.k[n], r.v[n])):
-            put_state(r.sloc, n, which, fold(tn(hi, rhs) + tn(lo, rhs)))
+        sums_of = [fold(tn(hi, rhs) + tn(lo, rhs)) for rhs in (r.k[n], r.v[n])]
+        for part in range(share_of):
+            lines = slice(part * third, part * third + third)
+            r.sloc[n * share_of + part, 0 : 3 * third, :] = pack_state(*[v[lines] for v in sums_of])
         r.info[pl.ds(n, 1), :] = jnp.sum(weight, axis=0, keepdims=True)
         return carry
 
@@ -423,7 +445,7 @@
 
     def spread(src, dst, info):
         for t in range(nch):
-            src[t, rows:, :] = info
+            src[t, src.shape[1] - 16 :, :] = info
         dst[chip] = src[chip]
         return [
             remote(src.at[lax.rem(chip + k, nch)], dst.at[chip], chip_device(lax.rem(chip + k, nch)))
@@ -438,7 +460,7 @@
         ]
 
     point()
-    out_1 = spread(r.sloc, r.rcv, r.info[...])
+    out_1 = spread(r.sloc, r.rcv, jnp.concatenate(halves(r.info[...]), axis=0))
 
     project(0)
 
@@ -464,26 +486,32 @@
     owned = (chip * rows) // 256
 
     def last_of(p, b):
-        return rcv[p, pl.ds(rows + 4 + b, 1), :]
+        return r.infos[p, pl.ds(4 + b, 1), :]
 
     def first_of(p, b):
-        return rcv[p, pl.ds(rows + 6 + b, 1), :]
-
-    run = jnp.zeros((rows, 128), F32)
+        return r.infos[p, pl.ds(6 + b, 1), :]
+
     for p in range(nch):
-        r.snd[p] = run
+        lines = rcv[p, 3 * third :, :].astype(F32)
+        r.infos[p] = lines[0:8] + lines[8:16]
+    run_k = jnp.zeros((third, 128), F32)
+    run_v = run_k
+    for p in range(nch):
+        r.snd[p] = pack_state(run_k, run_v)
+        got = rcv[p, 0 : 3 * third, :].astype(F32)
+        new_k, new_v = got[0:third] + got[third : 2 * third], got[2 * third :]
         if p == 0:
-            run = rcv[0, 0:rows, :]
+            run_k, run_v = new_k, new_v
         else:
             keep = (last_of(p - 1, owned) == last_of(p, owned)).astype(F32)
-            run = rcv[p, 0:rows, :] + keep * run
+            run_k, run_v = new_k + keep * run_k, new_v + keep * run_v
     point()
     out_2 = back(r.snd, r.stin)
     point()
     zrun = [jnp.zeros((2, 128), F32) for _ in range(SEQB)]
     for p in range(nch - 1):
         for b in range(SEQB):
-            z = rcv[p, rows + 2 * b : rows + 2 * b + 2, :]
+            z = r.infos[p, 2 * b : 2 * b + 2, :]
             if p > 0:
                 z = z + (last_of(p - 1, b) == last_of(p, b)).astype(F32) * zrun[b]
             zrun[b] = jnp.where(p < chip, z, zrun[b])
@@ -510,7 +538,7 @@
         b = n // 2
         q, v, whi = r.q[n], r.v[n], r.whi[n]
         mask, use = r.mask[b], r.use[b]
-        khi, klo = halves(get_block(r.stin, n, 0))
+        khi, klo = carried(n, 0), carried(n, 1)
         num = r.num[n] + use * (nt(q, khi) + nt(q, klo))
         tot = r.tot[n] + use * r.zin[pl.ds(n, 1), :]
         floor = jnp.maximum(tot, 1.0)
@@ -521,7 +549,7 @@
         r.score[n] = score
         r.share[n] = share
         sb = share.astype(BF)
-        out = use * nn(sb, get_block(r.stin, n, 1).astype(BF))
+        out = use * nn(sb, carried(n, 2))
         for m in hm:
             out += nn((nt(sb * m, whi) * mask).astype(BF), v * m)
         r.outb[n] = out.astype(BF).reshape(2, TOK, 128)
@@ -543,7 +571,7 @@
             [mixx[h, b * 2 + p] for h in range(2) for p in range(2)], axis=1
         )
     w_out = ago[...].reshape(512, 512)
-    residual = xv[...].reshape(256, 512).astype(F32) + nn(r.mixed[...], w_out)
+    residual = xall[:, core].reshape(256, 512).astype(F32) + nn(r.mixed[...], w_out)
     r.res[...] = residual
     unit, inv = norm_rows(residual)
     r.unit2[...] = unit
@@ -644,25 +672,23 @@
 
     load["dy"].wait()
     dy = dyv[...].reshape(256, 512)
-    span = na * OUTER // 4
+    blocks = [(j // 2, j % 2) if na == 2 else (0, j // 2, j % 2) for j in range(4)]
     for j in range(4):
         point()
         cols = slice(j * 512, j * 512 + 512)
-        pre = nn(r.n2[...], agu[:, :, :, :, :, cols].reshape(512, 512))
+        pre = nn(r.n2[...], agu[..., cols].reshape(512, 512))
         sig = 1.0 / (1.0 + jnp.exp(-pre))
         hidden = (pre * sig).astype(BF)
         r.hidden[:, cols] = hidden
         r.dsilu[:, cols] = sig * (1.0 + pre * (1.0 - sig))
-        block = (j * span // OUTER, slice(j * span % OUTER, j * span % OUTER + span))
-        r.gd[block] = tn(hidden, dy).astype(BF).reshape((span, ni, 2, 64, 512))
+        r.gd[blocks[j]] = tn(hidden, dy).astype(BF).reshape(lead[len(blocks[j]) :] + (64, 512))
     for j in range(4):
         point()
         cols = slice(j * 512, j * 512 + 512)
-        block = (j * span // OUTER, slice(j * span % OUTER, j * span % OUTER + span))
-        d_pre = (nt(dy, agd[block].reshape(512, 512)) * r.dsilu[:, cols]).astype(BF)
-        part = nt(d_pre, agu[:, :, :, :, :, cols].reshape(512, 512))
+        d_pre = (nt(dy, agd[blocks[j]].reshape(512, 512)) * r.dsilu[:, cols]).astype(BF)
+        part = nt(d_pre, agu[..., cols].reshape(512, 512))
         r.dn2[...] = part if j == 0 else r.dn2[...] + part
-        r.gu[:, :, :, :, :, cols] = nn(r.n2t[...], d_pre).astype(BF).reshape((na, OUTER, ni, 2, 16, 512))
+        r.gu[..., cols] = nn(r.n2t[...], d_pre).astype(BF).reshape(lead + (16, 512))
     point()
 
     dn2 = r.dn2[...]
@@ -690,7 +716,7 @@
         mask, use = r.mask[b], r.use[b]
         share, tot, score = r.share[n], r.tot[n], r.score[n]
         d_out = r.do[n].reshape(256, 128)
-        ds = use * nt(d_out, get_block(r.stin, n, 1).astype(BF))
+        ds = use * nt(d_out, carried(n, 2))
         for m in hm:
             ds += nn((nt(d_out * m, v) * mask).astype(BF), whi * m)
         floor = jnp.maximum(tot, 1.0)
@@ -715,19 +741,13 @@
     gz_parts = jnp.concatenate(halves(r.gz[...]), axis=0)
     out_3 = spread(r.dloc, r.drcv, gz_parts)
 
-    point()
-    r.go[...] = tn(r.mixed[...], d_attn).astype(BF).reshape((na, OUTER, ni, 2, 16, 512))
-    point()
-    y_rows = r.res[...] + nn(r.hidden[...], agd[...].reshape(FF, 512))
-    y_ref[...] = y_rows.astype(BF).reshape(SEQB, TOK, 512)
-
     def mix_back_local(n, carry):
         b = n // 2
         q, k, v, whi, w = r.q[n], r.k[n], r.v[n], r.whi[n], r.w[n]
         mask, maskt, use = r.mask[b], r.maskt[b], r.use[b]
         d_out, dnum = r.do[n].reshape(256, 128), r.dnum[n]
         sb = r.share[n].astype(BF)
-        dq = use * nn(dnum, get_block(r.stin, n, 0).astype(BF))
+        dq = use * nn(dnum, carried(n, 0))
         dk = jnp.zeros((256, 128), F32)
         dv = jnp.zeros((256, 128), F32)
         dw = nn(maskt.astype(BF), r.dtot[n].astype(BF))
@@ -750,10 +770,8 @@
 
     def weight_gradient(lo, width):
         value = nn(r.norm1t[...], dd[:, :, :, lo : lo + width].reshape(512, width))
-        r.gq[:, :, :, :, :, lo : lo + width] = value.astype(BF).reshape((na, OUTER, ni, 2, 16, width))
-
-    point()
-    weight_gradient(0, 256)
+        r.gq[..., lo : lo + width] = value.astype(BF).reshape(lead + (16, width))
+
     point()
 
     arrived(out_3)
@@ -784,43 +802,47 @@
         matched = (first_of(after, b) == r.info[4 + b : 5 + b, :]) & (chip < nch - 1)
         r.last[b] = r.last[b] * matched.astype(F32)
     point()
+    r.go[...] = tn(r.mixed[...], d_attn).astype(BF).reshape(lead + (16, 512))
+    point()
+    y_rows = r.res[...] + nn(r.hidden[...], agd[...].reshape(FF, 512))
+    y_ref[...] = y_rows.astype(BF).reshape(SEQB, TOK, 512)
+
+    point()
+    weight_gradient(0, 256)
+    point()
     arrived(out_4)
-    point()
-
-    def mix_last(n, carry):
-        b = n // 2
-        k, v, whi, w, last = r.k[n], r.v[n], r.whi[n], r.w[n], r.last[b]
-        gk = get_block(r.gin, n, 0).astype(BF)
-        gv = get_block(r.gin, n, 1).astype(BF)
-        dk = r.dkl[n] + last * nn(whi, gk)
-        dv = r.dvl[n] + last * nn(whi, gv)
-        dw = r.dwl[n] + last * (nt(k, gk) + nt(v, gv) + r.gz[pl.ds(n, 1), :])
-        for slot, value in ((1, dk), (2, dv), (3, dw * w)):
+
+    def mix_last(slot, value):
+        def one(n, carry):
             cols = pl.ds(pl.multiple_of(slot * 256 + lax.rem(n, 2) * 128, 128), 128)
-            dd[b, :, :, cols] = value.astype(BF).reshape(2, TOK, 128)
-        return carry
-
-    lax.fori_loop(0, 4, mix_last, 0)
-    for name, lo in (("kg", 256), ("vg", 512), ("cg", 768)):
+            dd[n // 2, :, :, cols] = value(n, r.last[n // 2]).astype(BF).reshape(2, TOK, 128)
+            return carry
+
         point()
-        weight_gradient(lo, 256)
+        lax.fori_loop(0, 4, one, 0)
+        point()
+        weight_gradient(slot * 256, 256)
+
+    def state_gradient(n, which):
+        return get_block(r.gin, n, which).astype(BF)
+
+    def weight_value(n, last):
+        more = nt(r.k[n], state_gradient(n, 0)) + nt(r.v[n], state_gradient(n, 1)) + r.gz[pl.ds(n, 1), :]
+        return (r.dwl[n] + last * more) * r.w[n]
+
+    mix_last(2, lambda n, last: r.dvl[n] + last * nn(r.whi[n], state_gradient(n, 1)))
+    mix_last(1, lambda n, last: r.dkl[n] + last * nn(r.whi[n], state_gradient(n, 0)))
+    mix_last(3, weight_value)
 
     point()
     full_q = agq[...].reshape(512, 1024)
+    gains1 = jnp.zeros((1, 512), F32)
     for b in range(SEQB):
         part = nt(dd[b].reshape(256, 1024), full_q)
         r.dn1[:, b] = part.reshape(2, TOK, 512)
+        gains1 += jnp.sum(part * r.unit1[b].reshape(256, 512), axis=0, keepdims=True)
     point()
     swap_g = remote(r.dn1.at[1 - core], r.dn1r, mate)
-
-    point()
-    swap_g.wait_recv()
-    point()
-    dn1 = (r.dn1[core] + r.dn1r[...]).reshape(256, 512)
-    unit = r.unit1[...]
-    gains1 = jnp.sum(dn1 * unit, axis=0, keepdims=True)
-    dx = r.dres[...] + norm_back(dn1 * ga_ref[...], unit, r.inv1[:, 0:1])
-    dx_ref[...] = dx.astype(BF).reshape(SEQB, TOK, 512)
 
     gains = jnp.concatenate(
         [g[:, j * 128 : j * 128 + 128] for g in (gains1, gains2) for j in range(4)], axis=0
@@ -839,6 +861,15 @@
 
     point()
     copies = exchange(r.gain1, gains, core, 2, lambda t: device(c=t))
+
+    point()
+    swap_g.wait_recv()
+    point()
+    dn1 = (r.dn1[core] + r.dn1r[...]).reshape(256, 512)
+    unit = r.unit1[:, core].reshape(256, 512)
+    dx = r.dres[...] + norm_back(dn1 * ga_ref[...], unit, r.inv1[:, core].reshape(256, 128)[:, 0:1])
+    dx_ref[...] = dx.astype(BF).reshape(SEQB, TOK, 512)
+
     point()
     gains = total(r.gain1, copies, 2)
     point()

time: 104 us -> 101 us (0.971)
  Pallas kernels: 103 us -> 99.7 us
    pallas_call x1, Pallas kernels: 101 us -> 97.6 us  [body(): pl.pallas_call(functools.partial(kernel, na, ni, names), out_shape=outs,...]
where the time goes in v3:
time: 101 us; the launch traced here: 100 us
  Pallas kernels  99.7 us (99%)
    pallas_call x1, Pallas kernels, body(): pl.pallas_call(functools.partial(kernel, na, ni, names), out_shape=outs,...  97.6 us
    pallas_call x1, Pallas kernels, body(): pl.pallas_call(functools.partial(hand_over, 11), out_shape=outs, in_specs...  2.08 us

profile of v3, /device:TPU:0, one launch (start us, length us, event | category | flops | bytes accessed | tf_op | source)
XLA Modules:
  0.0 100.4 jit_solution(5180925112510655120)
XLA Ops:
  0.6 97.6 %block.1 = (bf16[2,128,512]{2,1,0:T(8,128)(2,1)}, bf16[2,128,512]{2,1,0:T(8,128)(2,1)}, f32[64,128]{1,0:T(8,128)}, f32[64,128]{1,0:T(8,128)}, f32[64,128]{1,0:T(...) custom-call(bf16[2,128,512]{2,1,0:T(8,128)(2,1)} %refs_0_.1, ...), custom_call_target="tpu_custom_call" | custom-call | flops 12000000000 | bytes 4194304 | tf_op jit(solution)/shard_map/block/pallas_call | solution.py:934
  98.3 2.1 %results.1 = (bf16[2,128,512]{2,1,0:T(8,128)(2,1)}, bf16[2,128,512]{2,1,0:T(8,128)(2,1)}, f32[64,128]{1,0:T(8,128)}, f32[64,128]{1,0:T(8,128)}, f32[64,128]{1,0:...) custom-call(bf16[2,128,512]{2,1,0:T(8,128)(2,1)} %get-tuple-element., ...), custom_call_target="tpu_custom_call" | custom-call | tf_op jit(solution)/shard_map/results/pallas_call | solution.py:946

commit v4 on v3

--- a/solution.py
+++ b/solution.py
@@ -276,6 +276,13 @@
         for copy in copies:
             copy.wait_recv()
 
+    sent = [0]
+
+    def drain(count):
+        for copy in started[sent[0] : count]:
+            copy.wait_send()
+        sent[0] = count
+
     mate = device(c=1 - core)
 
     barrier = pltpu.get_barrier_semaphore()
@@ -319,10 +326,6 @@
             cols = slice(w * 256 + j * 128, w * 256 + j * 128 + 128)
             agq[own + (slice(None), cols)] = jnp.where(first_core, blk[j], blk[2 + j])
             r.sendq[:, cols] = jnp.where(first_core, blk[2 + j], blk[j])
-    for ref, buf, height, width in (("wo", ago, 16, 512), ("wu", agu, 16, FF), ("wd", agd, 64, 512)):
-        for j, blk in enumerate(unpack(ref, height, width)):
-            buf[own + (slice(None), slice(j * 128, j * 128 + 128))] = blk
-
     norm1 = r.norm1
     mini = r.mini
     mini[core, 0:2, :] = seg_ref[...].astype(F32)
@@ -344,6 +347,10 @@
             remote(ref, ref, device(**{axis: lax.rem(at[axis] + k, size[axis])}))
             for k in range(1, size[axis])
         ]
+
+    for ref, buf, height, width in (("wo", ago, 16, 512), ("wu", agu, 16, FF), ("wd", agd, 64, 512)):
+        for j, blk in enumerate(unpack(ref, height, width)):
+            buf[own + (slice(None), slice(j * 128, j * 128 + 128))] = blk
 
     swap_w.wait_recv()
     flying, done = {}, ["c" if part[0] == "agq" else "" for part in GATHER]
@@ -460,6 +467,7 @@
         ]
 
     point()
+    mark = len(started)
     out_1 = spread(r.sloc, r.rcv, jnp.concatenate(halves(r.info[...]), axis=0))
 
     project(0)
@@ -523,6 +531,7 @@
         r.use[b] = jnp.broadcast_to((seg_col == open_doc).astype(F32), (256, 128))
 
     point()
+    drain(mark)
     arrived(out_2)
 
     def both(op, v):
@@ -739,6 +748,7 @@
     point()
     r.gz[4:8, :] = jnp.zeros((4, 128), F32)
     gz_parts = jnp.concatenate(halves(r.gz[...]), axis=0)
+    mark = len(started)
     out_3 = spread(r.dloc, r.drcv, gz_parts)
 
     def mix_back_local(n, carry):
@@ -810,6 +820,7 @@
     point()
     weight_gradient(0, 256)
     point()
+    drain(mark)
     arrived(out_4)
 
     def mix_last(slot, value):
@@ -873,6 +884,7 @@
     point()
     gains = total(r.gain1, copies, 2)
     point()
+    mark = len(started)
     copies = exchange(r.gain2, gains, chip, nch, chip_device)
     point()
     gains = total(r.gain2, copies, nch)
@@ -888,13 +900,13 @@
         for j in range(4):
             ref[:, j * 128 : j * 128 + 128] = gains[first + j : first + j + 1]
     point()
+    drain(mark)
     swap_f.wait_recv()
     for ref, lo in ((oq_ref, 0), (ok_ref, 256), (ov_ref, 512), (oc_ref, 768)):
         for j in range(4):
             ref[pl.ds(j, 16, stride=4), :] = final[j // 2, :, lo + (j % 2) * 128 : lo + (j % 2) * 128 + 128]
     point()
-    for copy in started:
-        copy.wait_send()
+    drain(len(started))
 
 
 def hand_over(count, *refs):

time: 101 us -> 100 us (0.990)
  no operation moved by 1% of the time
where the time goes in v4:
time: 100 us
  Pallas kernels  99.5 us (100%)
    pallas_call x1, Pallas kernels, body(): pl.pallas_call(functools.partial(kernel, na, ni, names), out_shape=outs,...  97.4 us
    pallas_call x1, Pallas kernels, body(): pl.pallas_call(functools.partial(hand_over, 11), out_shape=outs, in_specs...  2.08 us

profile of v4, /device:TPU:0, one launch (start us, length us, event | category | flops | bytes accessed | tf_op | source)
XLA Modules:
  0.0 100.2 jit_solution(15463387109533034757)
XLA Ops:
  0.6 97.4 %block.1 = (bf16[2,128,512]{2,1,0:T(8,128)(2,1)}, bf16[2,128,512]{2,1,0:T(8,128)(2,1)}, f32[64,128]{1,0:T(8,128)}, f32[64,128]{1,0:T(8,128)}, f32[64,128]{1,0:T(...) custom-call(bf16[2,128,512]{2,1,0:T(8,128)(2,1)} %refs_0_.1, ...), custom_call_target="tpu_custom_call" | custom-call | flops 12000000000 | bytes 4194304 | tf_op jit(solution)/shard_map/block/pallas_call | solution.py:946
  98.1 2.1 %results.1 = (bf16[2,128,512]{2,1,0:T(8,128)(2,1)}, bf16[2,128,512]{2,1,0:T(8,128)(2,1)}, f32[64,128]{1,0:T(8,128)}, f32[64,128]{1,0:T(8,128)}, f32[64,128]{1,0:...) custom-call(bf16[2,128,512]{2,1,0:T(8,128)(2,1)} %get-tuple-element., ...), custom_call_target="tpu_custom_call" | custom-call | tf_op jit(solution)/shard_map/results/pallas_call | solution.py:958
